TPU v7x, 32 devices: a whole 2x2x4 slice. The times are simulated.
32 devices in a mesh: dp: 8 (over y, x, core), shard: 4 (over z).
Axes of the slice: x: 2, y: 2, z: 4, core: 2. Of those that a mesh axis runs over, the one named last changes fastest.
Arguments:
- hidden_in: bfloat16 [4, 1024, 8192], P('shard', 'dp'), may hold values from -600 to 600
- norm_gain: bfloat16 [8192], replicated, may hold values from 0.5 to 1.5
- key_weight: bfloat16 [8192, 512], P('shard'), may hold values from -0.0625 to 0.0625
- queries: bfloat16 [4, 1024, 4096], P('shard', 'dp'), may hold values from -100 to 100
- logp_grad: bfloat16 [4, 1024, 4096], P('shard', 'dp'), may hold values from -6 to 6
- values: bfloat16 [4, 1024, 512], P('shard', 'dp'), may hold values from -6 to 6
- advantages: float32 [4, 1024], P('shard', 'dp'), may hold values from -4 to 4
- log_ratio: float32 [4, 1024], P('shard', 'dp'), may hold values from -0.5 to 0.5
- resp_lengths: int32 [4, 8], P('shard'), may hold values from 1 to 512, 1024 in all within a row
- block_slots: int32 [4, 64], P('shard', 'dp'), may hold values from 0 to 63, as said below
Outputs:
- input_grad: bfloat16 [4, 1024, 8192], P('shard', 'dp')
- query_grad: bfloat16 [4, 1024, 4096], P('shard', 'dp')
- value_grad: bfloat16 [4, 1024, 512], P('shard', 'dp')
- key_weight_grad: float32 [8, 8192, 512], P('dp', 'shard')
- gain_grad: float32 [8, 8192], P('dp', 'shard')
Inputs may be any that keep to these rules, and one draw needn't show every extreme that they name: `resp_lengths`: row g lists the response lengths of stream g; they sum to 1024 and the longest is 512. `block_slots`: each row is a permutation of the 64 slots; slot // 8 is the index along dp whose balanced rows take the block. The 8 blocks of the rows of one device go to 8 different indices along dp, so one device sends at most one block to another.
All inputs are finite; a program needn't handle non-finite values.
Results may differ from a plain program's by a relative error of at most 0.025.
The roundings to bfloat16 on the way count: a program that leaves them out, or rounds other values in their place, can miss the bound.
Values may be sent and summed in bfloat16 or wider, within the bound.
A program may use at most 128 MiB of HBM per device.

v0:
```python
import math

import jax
import jax.numpy as jnp
from jax import lax
from jax.sharding import PartitionSpec as P

HD = 128
QH = 32
KVH = 4


norm_eps = 1e-05
rope_base = 500000.0
upper_log = math.log(1.2)
lower_log = math.log(0.8)
masked_score = -1e30


def rope_tables(positions, head_size):
    half_size = head_size // 2
    frequency = rope_base ** (-(jnp.arange(half_size, dtype=jnp.float32) * 2.0) / head_size)
    angles = positions.astype(jnp.float32)[:, None] * frequency[None, :]
    return (jnp.cos(angles)[:, None, :], jnp.sin(angles)[:, None, :])


def rotate(tensor, cosine_table, sine_table):
    half_size = tensor.shape[-1] // 2
    first_half = tensor[..., :half_size]
    second_half = tensor[..., half_size:]
    return jnp.concatenate(
        [
            first_half * cosine_table - second_half * sine_table,
            second_half * cosine_table + first_half * sine_table,
        ],
        axis=-1,
    )


def rotate_back(tensor, cosine_table, sine_table):
    half_size = tensor.shape[-1] // 2
    first_half = tensor[..., :half_size]
    second_half = tensor[..., half_size:]
    return jnp.concatenate(
        [
            first_half * cosine_table + second_half * sine_table,
            second_half * cosine_table - first_half * sine_table,
        ],
        axis=-1,
    )


def segment_info(lengths, row_ids):
    seg_ends = jnp.cumsum(lengths)
    starts = seg_ends - lengths
    inside = (row_ids[:, None] >= starts[None, :]) & (row_ids[:, None] < seg_ends[None, :])
    labels = jnp.arange(lengths.shape[0], dtype=jnp.int32)
    segment = jnp.sum(jnp.where(inside, labels[None, :], 0), axis=1)
    seg_begin = jnp.sum(jnp.where(inside, starts[None, :], 0), axis=1)
    return (segment, row_ids - seg_begin)


def token_weight(advantage, ratio_log):
    keep_mask = jnp.where(advantage >= 0.0, ratio_log <= upper_log, ratio_log >= lower_log)
    return jnp.where(keep_mask, -advantage * jnp.exp(ratio_log), 0.0)


def keep_state(state):
    return state


def attend_blocks(
    query_bal, grad_bal, query_index, query_segment, stream_keys, stream_values, key_segment
):
    row_count = query_bal.shape[0]
    stream_len = stream_keys.shape[0]
    groups = QH // KVH
    block_len = min(256, stream_len)
    block_count = stream_len // block_len
    score_scale = 1.0 / math.sqrt(HD)
    query_heads = query_bal.reshape(row_count, KVH, groups, HD)
    grad_heads = grad_bal.reshape(row_count, KVH, groups, HD)
    key_heads = stream_keys.reshape(stream_len, KVH, HD)
    value_heads = stream_values.reshape(stream_len, KVH, HD)

    def block_mask(index):
        start = index * block_len
        seg_block = lax.dynamic_slice_in_dim(key_segment, start, block_len, 0)
        key_index = start + jnp.arange(block_len, dtype=jnp.int32)
        return (query_segment[:, None] == seg_block[None, :]) & (
            key_index[None, :] <= query_index[:, None]
        )

    def block_keys(index):
        return lax.dynamic_slice_in_dim(key_heads, index * block_len, block_len, 0)

    def block_values(index):
        return lax.dynamic_slice_in_dim(value_heads, index * block_len, block_len, 0)

    def block_scores(index, allowed):
        scores = (
            jnp.einsum(
                "tkgd,jkd->kgtj", query_heads, block_keys(index), preferred_element_type=jnp.float32
            )
            * score_scale
        )
        return jnp.where(allowed, scores, masked_score)

    def guarded(allowed, compute, state):
        return lax.cond(jnp.any(allowed), compute, keep_state, state)

    def stats_step(index, state):
        allowed = block_mask(index)

        def compute(inner):
            row_max, row_sum = inner
            scores = block_scores(index, allowed)
            new_max = jnp.maximum(row_max, jnp.max(scores, axis=-1))
            exp_terms = jnp.where(allowed, jnp.exp(scores - new_max[..., None]), 0.0)
            return (new_max, row_sum * jnp.exp(row_max - new_max) + jnp.sum(exp_terms, axis=-1))

        return guarded(allowed, compute, state)

    start_max = jnp.full((KVH, groups, row_count), masked_score, jnp.float32)
    start_sum = jnp.zeros((KVH, groups, row_count), jnp.float32)
    row_max, row_sum = lax.fori_loop(0, block_count, stats_step, (start_max, start_sum))

    def soft_weights(index, allowed):
        scores = block_scores(index, allowed)
        return jnp.where(allowed, jnp.exp(scores - row_max[..., None]), 0.0) / row_sum[..., None]

    def output_step(index, state):
        allowed = block_mask(index)

        def compute(total):
            weights_b = soft_weights(index, allowed).astype(jnp.bfloat16)
            return total + jnp.einsum(
                "kgtj,jkd->tkgd", weights_b, block_values(index), preferred_element_type=jnp.float32
            )

        return guarded(allowed, compute, state)

    attn_out = lax.fori_loop(
        0, block_count, output_step, jnp.zeros((row_count, KVH, groups, HD), jnp.float32)
    )
    row_delta = jnp.einsum(
        "tkgd,tkgd->kgt", grad_heads, attn_out, preferred_element_type=jnp.float32
    )

    def grad_step(index, state):
        allowed = block_mask(index)

        def compute(inner):
            query_acc, key_acc, value_acc = inner
            weights_f = soft_weights(index, allowed)
            weights_b = weights_f.astype(jnp.bfloat16)
            key_block = block_keys(index)
            prob_grad = jnp.einsum(
                "tkgd,jkd->kgtj",
                grad_heads,
                block_values(index),
                preferred_element_type=jnp.float32,
            )
            score_grad = (weights_f * (prob_grad - row_delta[..., None])).astype(jnp.bfloat16)
            query_acc = query_acc + jnp.einsum(
                "kgtj,jkd->tkgd", score_grad, key_block, preferred_element_type=jnp.float32
            )
            key_part = (
                jnp.einsum(
                    "kgtj,tkgd->jkd", score_grad, query_heads, preferred_element_type=jnp.float32
                )
                * score_scale
            )
            value_part = jnp.einsum(
                "kgtj,tkgd->jkd", weights_b, grad_heads, preferred_element_type=jnp.float32
            )
            key_acc = lax.dynamic_update_slice_in_dim(key_acc, key_part, index * block_len, 0)
            value_acc = lax.dynamic_update_slice_in_dim(value_acc, value_part, index * block_len, 0)
            return (query_acc, key_acc, value_acc)

        return guarded(allowed, compute, state)

    start_grads = (
        jnp.zeros((row_count, KVH, groups, HD), jnp.float32),
        jnp.zeros((stream_len, KVH, HD), jnp.float32),
        jnp.zeros((stream_len, KVH, HD), jnp.float32),
    )
    query_acc, key_acc, value_acc = lax.fori_loop(0, block_count, grad_step, start_grads)
    query_grad = (query_acc * score_scale).astype(jnp.bfloat16).reshape(row_count, QH * HD)
    return (query_grad, key_acc, value_acc)


def local(
    hidden_in,
    norm_gain,
    key_weight,
    queries,
    logp_grad,
    values,
    advantages,
    log_ratio,
    resp_lengths,
    block_slots,
):
    row_count = hidden_in.shape[1]
    dp_size = lax.axis_size("dp")
    stream_len = row_count * dp_size
    blocks_dev = block_slots.shape[1]
    block_rows = row_count // blocks_dev
    key_width = key_weight.shape[1]
    query_width = queries.shape[2]
    here = lax.axis_index("dp")
    row_ids = here * row_count + jnp.arange(row_count, dtype=jnp.int32)
    lengths = resp_lengths[0]
    segment, position = segment_info(lengths, row_ids)
    x_float = hidden_in[0].astype(jnp.float32)
    inv_rms = lax.rsqrt(jnp.mean(x_float * x_float, axis=1, keepdims=True) + norm_eps)
    normed = x_float * inv_rms
    gain_f = norm_gain.astype(jnp.float32)
    normed_in = (normed * gain_f[None, :]).astype(jnp.bfloat16)
    full_weight = lax.all_gather(key_weight, "shard", axis=0, tiled=True)
    raw_keys = jnp.dot(normed_in, full_weight, preferred_element_type=jnp.float32)
    cosine_table, sine_table = rope_tables(position, HD)
    key_rows = (
        rotate(raw_keys.reshape(row_count, KVH, HD), cosine_table, sine_table)
        .astype(jnp.bfloat16)
        .reshape(row_count, key_width)
    )
    weight_tok = token_weight(advantages[0], log_ratio[0])
    out_grad = (weight_tok[:, None] * logp_grad[0].astype(jnp.float32)).astype(jnp.bfloat16)
    stream_keys, stream_values = (
        lax.all_gather(key_rows, "dp", axis=0, tiled=True),
        lax.all_gather(values[0], "dp", axis=0, tiled=True),
    )
    slot_list = block_slots[0]
    dest_dev = slot_list // blocks_dev
    pick_send = (dest_dev[None, :] == jnp.arange(dp_size, dtype=jnp.int32)[:, None]).astype(
        jnp.bfloat16
    )
    payload = jnp.concatenate([queries[0], out_grad], axis=1).reshape(
        blocks_dev, block_rows * 2 * query_width
    )
    outgoing = (
        jnp.dot(pick_send, payload, preferred_element_type=jnp.float32)
        .astype(jnp.bfloat16)
        .reshape(dp_size, block_rows, 2 * query_width)
    )
    incoming = lax.all_to_all(outgoing, "dp", split_axis=0, concat_axis=0, tiled=True)
    slot_table = lax.all_gather(slot_list, "dp", axis=0, tiled=True)
    my_slots = here * blocks_dev + jnp.arange(blocks_dev, dtype=jnp.int32)
    all_blocks = jnp.arange(slot_table.shape[0], dtype=jnp.int32)
    source_block = jnp.sum(
        jnp.where(slot_table[None, :] == my_slots[:, None], all_blocks[None, :], 0), axis=1
    )
    source_dev = source_block // blocks_dev
    pick_recv = (source_dev[:, None] == jnp.arange(dp_size, dtype=jnp.int32)[None, :]).astype(
        jnp.bfloat16
    )
    arranged = (
        jnp.dot(
            pick_recv,
            incoming.reshape(dp_size, block_rows * 2 * query_width),
            preferred_element_type=jnp.float32,
        )
        .astype(jnp.bfloat16)
        .reshape(row_count, 2 * query_width)
    )
    query_bal = arranged[:, :query_width]
    grad_bal = arranged[:, query_width:]
    query_index = (
        source_block[:, None] * block_rows + jnp.arange(block_rows, dtype=jnp.int32)[None, :]
    ).reshape(row_count)
    key_segment = segment_info(lengths, jnp.arange(stream_len, dtype=jnp.int32))[0]
    query_segment = jnp.take(key_segment, query_index)
    query_grad, key_acc, value_acc = attend_blocks(
        query_bal, grad_bal, query_index, query_segment, stream_keys, stream_values, key_segment
    )
    key_sum, value_sum = (
        lax.psum_scatter(
            key_acc.reshape(stream_len, key_width).astype(jnp.bfloat16),
            "dp",
            scatter_dimension=0,
            tiled=True,
        ).astype(jnp.float32),
        lax.psum_scatter(
            value_acc.reshape(stream_len, key_width).astype(jnp.bfloat16),
            "dp",
            scatter_dimension=0,
            tiled=True,
        ).astype(jnp.float32),
    )
    value_grad = value_sum.astype(jnp.bfloat16)
    raw_grad = (
        rotate_back(key_sum.reshape(row_count, KVH, HD), cosine_table, sine_table)
        .astype(jnp.bfloat16)
        .reshape(row_count, key_width)
    )
    normed_grad = jnp.einsum(
        "rk,ck->rc", raw_grad, full_weight, preferred_element_type=jnp.float32
    ).astype(jnp.bfloat16)
    grad_f = normed_grad.astype(jnp.float32)
    weight_term = jnp.einsum("td,tk->dk", normed_in, raw_grad, preferred_element_type=jnp.float32)
    weight_grad, gain_grad = (
        lax.psum_scatter(
            weight_term.astype(jnp.bfloat16), "shard", scatter_dimension=0, tiled=True
        ).astype(jnp.float32),
        lax.psum_scatter(
            jnp.sum(grad_f * normed, axis=0).astype(jnp.bfloat16),
            "shard",
            scatter_dimension=0,
            tiled=True,
        ).astype(jnp.float32),
    )
    scaled = grad_f * gain_f[None, :]
    input_grad = (
        inv_rms * (scaled - normed * jnp.mean(scaled * normed, axis=1, keepdims=True))
    ).astype(jnp.bfloat16)
    return (
        input_grad[None],
        query_grad[None],
        value_grad[None],
        weight_grad[None],
        gain_grad[None],
    )


def solution(mesh):
    placed = (
        P("shard", "dp", None),
        P(),
        P("shard", None),
        P("shard", "dp", None),
        P("shard", "dp", None),
        P("shard", "dp", None),
        P("shard", "dp"),
        P("shard", "dp"),
        P("shard", None),
        P("shard", "dp"),
    )
    return jax.shard_map(
        local,
        mesh=mesh,
        in_specs=placed,
        out_specs=(
            P("shard", "dp", None),
            P("shard", "dp", None),
            P("shard", "dp", None),
            P("dp", "shard", None),
            P("dp", "shard"),
        ),
        check_vma=False,
    )
```

profile of v0, /device:TPU:0, one launch (start us, length us, event | category | flops | bytes accessed | tf_op | source)
XLA Modules:
  0.0 548.2 jit_solution(253125210784444767)
XLA Ops:
  17.4 5.2 all-to-all-start
  25.0 26.4 %all-reduce = s32[64]{0:T(128)S(1)} all-reduce(s32[64]{0:T(128)S(1)} %bitcast_dynamic-update-slice_fusion), channel_id=2, replica_groups=mesh['dp'=8,'shard'=4] {'dp'}, use_global_device_ids=true, to_apply=%add | all-reduce | flops 64 | bytes 512
  52.6 109.3 %all-gather.6.cloned.1.call-done = bf16[8192,512]{1,0:T(8,128)(2,1)} async-done(((bf16[2048,512]{1,0:T(8,128)(2,1)}), bf16[8192,512]{1,0:T(8,128)(2,1)}) %all-gather.6.cloned.1.call-update) | async-done | bytes 8388624 | tf_op jit(solution)/shard_map/all_gather | solution.py:221
  161.9 11.9 %copy.62 = bf16[512,8192]{1,0:T(8,128)(2,1)} copy(bf16[512,8192]{0,1:T(8,128)(2,1)} %bitcast.197) | data formatting | bytes 16777216 | tf_op jit(solution)/shard_map/dot_general | solution.py:222
  173.8 5.8 %fusion.70 = f32[128,4,128]{0,2,1:T(8,128)S(1)} fusion(bf16[4,128,8192]{2,1,0:T(8,128)(2,1)} %bitcast.198, bf16[1,128,8192]{2,1,0:T(8,128)(2,1)S(1)} %copy-done.2, f32[8192]{0:T(1024)S(1)} %convert_element_type.131, f32[128]{0:T(128)S(1)} %add_rsqrt_fusion), kind=kOutput, calls=%fused_computation.89 | convolution fusion | flops 1077936128 | bytes 10781184 | tf_op jit(solution)/shard_map/dot_general | solution.py:222
  196.4 15.9 %all-gather.8.cloned.1.call-done = bf16[1024,512]{0,1:T(8,128)(2,1)} async-done(((bf16[128,512]{0,1:T(8,128)(2,1)}), bf16[1024,512]{0,1:T(8,128)(2,1)}) %all-gather.8.cloned.1.call-update) | async-done | bytes 1048592 | tf_op jit(solution)/shard_map/all_gather | solution.py:232
  214.0 14.3 %while.51 = (s32[]{:T(128)}, f32[4,8,128]{2,1,0:T(8,128)S(1)}, f32[4,8,128]{2,1,0:T(8,128)S(1)}, s32[128]{0:T(128)S(1)}, s32[1024]{0:T(1024)S(1)}, /*index=5*/bf...) while((s32[]{:T(128)}, f32[4,8,128]{2,1,0:T(8,128)S(1)}, ...), condition=%wide.region_11.12_spmd.clone, body=%wide.region_5.11_spmd.clone.sunk | while | flops 276963712 | bytes 10018651 | solution.py:126
  229.9 26.0 %while.52 = (s32[]{:T(128)}, f32[128,4,8,128]{0,3,2,1:T(8,128)}, s32[128]{0:T(128)S(1)}, s32[1024]{0:T(1024)S(1)}, bf16[1024,4,128]{0,2,1:T(8,128)(2,1)}, /*inde...) while((s32[]{:T(128)}, f32[128,4,8,128]{0,3,2,1:T(8,128)}, ...), condition=%wide.region_16.17_spmd.clone, body=%wide.region_12.16_spmd.clone.sunk | while | flops 543818112 | bytes 5874519 | solution.py:143
  231.5 4.8 conditional.10
  238.0 4.8 conditional.10
  244.5 4.8 conditional.10
  251.0 4.8 conditional.10
  251.0 4.8 bitcast_add_fusion
  261.8 46.8 %while.53 = (s32[]{:T(128)}, f32[128,4,8,128]{0,3,2,1:T(8,128)S(1)}, bf16[1024,4,128]{2,0,1:T(8,128)(2,1)}, bf16[1024,4,128]{2,0,1:T(8,128)(2,1)}, s32[128]{0:T(...) while((s32[]{:T(128)}, ...), condition=%wide.region_21.22_spmd.clone, body=%wide.region_17.21_spmd.clone.sunk | while | flops 1352401280 | bytes 50192484 | solution.py:188
  263.4 10.0 %conditional.11 = ((f32[128,4,8,128]{0,3,2,1:T(8,128)S(1)}, bf16[1024,4,128]{2,0,1:T(8,128)(2,1)}, bf16[1024,4,128]{2,0,1:T(8,128)(2,1)})) conditional(s32[]{:T(128)} %convert_element_type.231, (f32[128,4,8,128]{0,3,2,1:T(8,128)S(1)}, bf16[1024,4,128]{2,0,1:T(8,128)(2,1)}, bf16[1024,4,128]{2,0,1:T(8,128)(2,1)}) %tuple.151, (s32[]{:T(128)}, ...), branch_computations={%region_19.19_spmd, %region_20.20_spmd} | conditional | flops 1352269824 | bytes 50151660 | solution.py:110
  275.1 10.1 %conditional.11 = ((f32[128,4,8,128]{0,3,2,1:T(8,128)S(1)}, bf16[1024,4,128]{2,0,1:T(8,128)(2,1)}, bf16[1024,4,128]{2,0,1:T(8,128)(2,1)})) conditional(s32[]{:T(128)} %convert_element_type.231, (f32[128,4,8,128]{0,3,2,1:T(8,128)S(1)}, bf16[1024,4,128]{2,0,1:T(8,128)(2,1)}, bf16[1024,4,128]{2,0,1:T(8,128)(2,1)}) %tuple.151, (s32[]{:T(128)}, ...), branch_computations={%region_19.19_spmd, %region_20.20_spmd} | conditional | flops 1352269824 | bytes 50151660 | solution.py:110
  286.8 10.1 %conditional.11 = ((f32[128,4,8,128]{0,3,2,1:T(8,128)S(1)}, bf16[1024,4,128]{2,0,1:T(8,128)(2,1)}, bf16[1024,4,128]{2,0,1:T(8,128)(2,1)})) conditional(s32[]{:T(128)} %convert_element_type.231, (f32[128,4,8,128]{0,3,2,1:T(8,128)S(1)}, bf16[1024,4,128]{2,0,1:T(8,128)(2,1)}, bf16[1024,4,128]{2,0,1:T(8,128)(2,1)}) %tuple.151, (s32[]{:T(128)}, ...), branch_computations={%region_19.19_spmd, %region_20.20_spmd} | conditional | flops 1352269824 | bytes 50151660 | solution.py:110
  298.5 10.1 %conditional.11 = ((f32[128,4,8,128]{0,3,2,1:T(8,128)S(1)}, bf16[1024,4,128]{2,0,1:T(8,128)(2,1)}, bf16[1024,4,128]{2,0,1:T(8,128)(2,1)})) conditional(s32[]{:T(128)} %convert_element_type.231, (f32[128,4,8,128]{0,3,2,1:T(8,128)S(1)}, bf16[1024,4,128]{2,0,1:T(8,128)(2,1)}, bf16[1024,4,128]{2,0,1:T(8,128)(2,1)}) %tuple.151, (s32[]{:T(128)}, ...), branch_computations={%region_19.19_spmd, %region_20.20_spmd} | conditional | flops 1352269824 | bytes 50151660 | solution.py:110
  311.5 36.1 %reduce-scatter.10.cloned.1.call-done = bf16[128,512]{1,0:T(8,128)(2,1)} async-done(((bf16[1024,512]{1,0:T(8,128)(2,1)}), bf16[128,512]{1,0:T(8,128)(2,1)}) %reduce-scatter.10.cloned.1.call-update) | async-done | bytes 131088
  348.7 7.3 %convolution_convert_fusion.2 = bf16[8192,512]{1,0:T(8,128)(2,1)} fusion(bf16[128,512]{0,1:T(8,128)(2,1)S(1)} %bitcast.208, bf16[1,128,8192]{2,1,0:T(8,128)(2,1)} %param.22, f32[8192]{0:T(1024)S(1)} %convert_element_type.131, f32[128]{0:T(128)S(1)} %add_rsqrt_fusion), kind=kOutput, calls=%fused_computation.64 | convolution fusion | flops 1082130432 | bytes 10650112 | tf_op jit(solution)/shard_map/td,tk->dk/dot_general | solution.py:302
  364.2 6.9 %fusion.63 = (bf16[8192]{0:T(1024)(128)(2,1)S(1)}, f32[128]{0:T(128)S(1)}, f32[128,8192]{1,0:T(8,128)S(1)}) fusion(bf16[1,128,8192]{2,1,0:T(8,128)(2,1)S(1)} %copy-done.3, f32[128]{0:T(128)S(1)} %add_rsqrt_fusion, f32[8192]{0:T(1024)S(1)} %convert_element_type.131, bf16[128,512]{0,1:T(8,128)(2,1)S(1)} %bitcast.209, ...), kind=kOutput, calls=%fused_computation.78 | convolution fusion | flops 1083170688 | bytes 14861312 | tf_op jit(solution)/shard_map/rk,ck->rc/dot_general | solution.py:298
  373.5 19.6 %all-reduce.1 = bf16[8192]{0:T(1024)(128)(2,1)S(1)} all-reduce(bf16[8192]{0:T(1024)(128)(2,1)S(1)} %get-tuple-element.846), channel_id=7, replica_groups=mesh['dp'=8,'shard'=4] {'shard'}, use_global_device_ids=true, to_apply=%region_27.28.clone | all-reduce | flops 8192 | bytes 32768
  393.6 107.5 %reduce-scatter.8.cloned.1.call-done = bf16[2048,512]{1,0:T(8,128)(2,1)} async-done(((bf16[8192,512]{1,0:T(8,128)(2,1)}), bf16[2048,512]{1,0:T(8,128)(2,1)}) %reduce-scatter.8.cloned.1.call-update) | async-done | bytes 2097168 | tf_op jit(solution)/shard_map/reduce_scatter | solution.py:304
  505.3 36.1 %reduce-scatter.6.cloned.1.call-done = bf16[128,512]{1,0:T(8,128)(2,1)} async-done(((bf16[1024,512]{1,0:T(8,128)(2,1)}), bf16[128,512]{1,0:T(8,128)(2,1)}) %reduce-scatter.6.cloned.1.call-update) | async-done | bytes 131088 | tf_op jit(solution)/shard_map/reduce_scatter | solution.py:285
  (250 shorter events, 138.6 us)
Async XLA Ops:
  7.2 2.9 copy-start.10
  7.2 154.8 %all-gather.6.cloned.1.call-start = ((), (), s32[]{:S(2)}) async-start(), calls=%async_computation.4 | async-start | bytes 10485760 | tf_op jit(solution)/shard_map/all_gather | solution.py:221
  10.1 4.0 copy-start.14
  14.8 7.8 %copy-start.11 = (bf16[1,128,512]{2,1,0:T(8,128)(2,1)S(1)}, bf16[1,128,512]{2,1,0:T(8,128)(2,1)}, u32[]{:S(2)}) copy-start(bf16[1,128,512]{2,1,0:T(8,128)(2,1)} %param.27) | copy-start | bytes 393220
  14.9 8.6 %copy-start.13 = (s32[1,8]{1,0:T(1,128)S(1)}, s32[1,8]{1,0:T(1,128)}, u32[]{:S(2)}) copy-start(s32[1,8]{1,0:T(1,128)} %param.30) | copy-start | bytes 100
  14.9 8.8 %copy-start.16 = (u32[32]{0:T(128)S(1)}, u32[32]{0:T(128)}, u32[]{:S(2)}) copy-start(u32[32]{0:T(128)} %constant.232) | copy-start | bytes 388
  14.9 36.9 %copy-start.12 = (bf16[8192]{0:T(1024)(128)(2,1)S(1)}, bf16[8192]{0:T(1024)(128)(2,1)}, u32[]{:S(2)}) copy-start(bf16[8192]{0:T(1024)(128)(2,1)} %param.23) | copy-start | bytes 49156
  14.9 37.2 %copy-start.2 = (bf16[1,128,8192]{2,1,0:T(8,128)(2,1)S(1)}, bf16[1,128,8192]{2,1,0:T(8,128)(2,1)}, u32[]{:S(2)}) copy-start(bf16[1,128,8192]{2,1,0:T(8,128)(2,1)} %param.22) | copy-start | bytes 6291460
  17.4 164.4 %all-to-all-start = ((bf16[8,16,8192]{2,1,0:T(8,128)(2,1)}), bf16[8,16,8192]{2,1,0:T(8,128)(2,1)}, u32[]{:S(2)}, u32[]{:S(2)}) async-start(bf16[8,16,8192]{2,1,0:T(8,128)(2,1)} %copy.63), calls=%async_computation | async-start | bytes 4194304 | tf_op jit(solution)/shard_map/all_to_all | solution.py:248
  22.6 171.5 %all-gather.10.cloned.1.call-start = ((), (), s32[]{:S(2)}) async-start(), calls=%async_computation.8 | async-start | bytes 1179648 | tf_op jit(solution)/shard_map/all_gather | solution.py:233
  23.4 188.9 %all-gather.8.cloned.1.call-start = ((), (), s32[]{:S(2)}) async-start(), calls=%async_computation.5 | async-start | bytes 1179648 | tf_op jit(solution)/shard_map/all_gather | solution.py:232
  180.4 167.2 %reduce-scatter.10.cloned.1.call-start = ((), (), s32[]{:S(2)}) async-start(), calls=%async_computation.9 | async-start | bytes 1179648
  193.4 19.0 %copy-start.5 = (bf16[128,4096]{0,1:T(8,128)(2,1)}, bf16[128,4096]{0,1:T(8,128)(2,1)S(1)}, u32[]{:S(2)}) copy-start(bf16[128,4096]{0,1:T(8,128)(2,1)S(1)} %copy.101) | copy-start | bytes 3145732
  267.7 2.1 copy-start.1
  267.8 2.1 copy-start.6
  279.5 2.1 copy-start.1
  279.5 2.1 copy-start.6
  291.2 2.1 copy-start.1
  291.2 2.1 copy-start.6
  302.9 2.1 copy-start.1
  302.9 2.1 copy-start.6
  311.4 189.7 %reduce-scatter.8.cloned.1.call-start = ((), (), s32[]{:S(2)}) async-start(), calls=%async_computation.7 | async-start | bytes 10485760 | tf_op jit(solution)/shard_map/reduce_scatter | solution.py:304
  356.0 185.4 %reduce-scatter.6.cloned.1.call-start = ((), (), s32[]{:S(2)}) async-start(), calls=%async_computation.6 | async-start | bytes 1179648 | tf_op jit(solution)/shard_map/reduce_scatter | solution.py:285
  359.1 5.1 copy-start.3
  (15 other events, 18.1 us)
Sparse Core Ops, SparseCore 0:
  9.6 152.3 all-gather.5
  164.4 21.8 all-gather.9
  188.7 23.5 all-gather.7
  311.5 35.9 reduce-scatter.9
  356.1 144.9 reduce-scatter.7
  504.7 36.6 reduce-scatter.5
where the time goes:
time: 550 us; the launch traced here: 548 us
  waiting for transfers between devices  306 us (56%)
  matrix products  76.9 us (14%)
  local copies, waits for them, and re-layouts  58.7 us (11%)
  blocking collectives  46 us (8%)
  other arithmetic  30.9 us (6%)
  between operations  15.8 us (3%)
  loops' own time  8.72 us (2%)
  starting transfers between devices  5.59 us (1%)
    all_gather x1, waiting for transfers between devices, local(): full_weight = lax.all_gather(key_weight, 'shard', axis=0, tiled=True)  109 us
    reduce_scatter x1, waiting for transfers between devices, local(): lax.psum_scatter(weight_term.astype(jnp.bfloat16), 'shard', scatter_dimen...  107 us
    unnamed x2, blocking collectives  46 us
    unnamed x7, waiting for transfers between devices  36.9 us
    reduce_scatter x1, waiting for transfers between devices, local(): lax.psum_scatter(value_acc.reshape(stream_len, key_width).astype(jnp.bflo...  36.1 us
    dot_general x4, matrix products, compute(): jnp.einsum('kgtj,jkd->tkgd', weights_b, block_values(index), preferred_el...  19.2 us
    unnamed x38, local copies, waits for them, and re-layouts  16.7 us
    all_gather x1, waiting for transfers between devices, local(): lax.all_gather(key_rows, 'dp', axis=0, tiled=True)  15.9 us
  transfers between devices with their start and end apart: 7, of which 5 were waited for; matrix products, arithmetic and copies ran while one was open for 12% of the time, Pallas kernels for 0%

commit v1 on v0

v1 whole, which is shorter than its diff:
```python
import functools
import math

import jax
import jax.numpy as jnp
from jax import lax
from jax.experimental import pallas as pl
from jax.experimental.pallas import tpu as pltpu
from jax.sharding import PartitionSpec as P

HD = 128
QH = 32
KVH = 4
GROUPS = QH // KVH

norm_eps = 1e-05
rope_base = 500000.0
upper_log = math.log(1.2)
lower_log = math.log(0.8)
masked_score = -1e30
MESH = pl.DeviceIdType.MESH
F32 = jnp.float32
BF16 = jnp.bfloat16


def rope_tables(positions, head_size):
    half_size = head_size // 2
    frequency = rope_base ** (-(jnp.arange(half_size, dtype=F32) * 2.0) / head_size)
    angles = positions.astype(F32)[:, None] * frequency[None, :]
    return (jnp.cos(angles)[:, None, :], jnp.sin(angles)[:, None, :])


def rotate(tensor, cosine_table, sine_table):
    half_size = tensor.shape[-1] // 2
    a = tensor[..., :half_size]
    b = tensor[..., half_size:]
    return jnp.concatenate(
        [a * cosine_table - b * sine_table, b * cosine_table + a * sine_table], axis=-1
    )


def segment_starts(lengths, row_ids):
    seg_ends = jnp.cumsum(lengths)
    starts = seg_ends - lengths
    inside = (row_ids[:, None] >= starts[None, :]) & (row_ids[:, None] < seg_ends[None, :])
    return jnp.sum(jnp.where(inside, starts[None, :], 0), axis=1)


def token_weight(advantage, ratio_log):
    keep_mask = jnp.where(advantage >= 0.0, ratio_log <= upper_log, ratio_log >= lower_log)
    return jnp.where(keep_mask, -advantage * jnp.exp(ratio_log), 0.0)


def exchange_kernel(axis, n, modes, with_weight, n_shard, *refs):
    count = len(modes)
    ins = refs[: count + with_weight]
    outs = refs[count + with_weight : 2 * (count + with_weight)]
    rest = refs[2 * (count + with_weight) :]
    send_sem, recv_sem, local_sem = rest[:3]
    me = lax.axis_index(axis)
    barrier = pltpu.get_barrier_semaphore()
    for k in range(1, n):
        pl.semaphore_signal(
            barrier, inc=1, device_id={axis: lax.rem(me + k, n)}, device_id_type=MESH
        )
    greeted = n - 1
    if with_weight:
        z = lax.axis_index("shard")
        for k in range(1, n_shard):
            pl.semaphore_signal(
                barrier, inc=1, device_id={"shard": lax.rem(z + k, n_shard)}, device_id_type=MESH
            )
        greeted += n_shard - 1
    pl.semaphore_wait(barrier, greeted)

    w_copies = []
    if with_weight:
        wsend, wrecv, fsend, frecv, wloc = rest[3:]
        w_in, w_out = ins[count], outs[count]
        rows = w_in.shape[0]
        half_rows = rows // 2
        half = lax.rem(me, 2)
        mine = pl.ds(pl.multiple_of(half * half_rows, half_rows), half_rows)
        for k in range(1, n_shard):
            c = pltpu.make_async_remote_copy(
                src_ref=w_in.at[mine],
                dst_ref=w_out.at[z, mine],
                send_sem=wsend.at[k],
                recv_sem=wrecv.at[k],
                device_id={"shard": lax.rem(z + k, n_shard)},
                device_id_type=MESH,
            )
            c.start()
            w_copies.append(c)
    copies = []
    for a, mode in enumerate(modes):
        for k in range(1, n):
            peer = lax.rem(me + k, n)
            c = pltpu.make_async_remote_copy(
                src_ref=ins[a].at[peer] if mode == "a2a" else ins[a],
                dst_ref=outs[a].at[me],
                send_sem=send_sem.at[a, k],
                recv_sem=recv_sem.at[a, k],
                device_id={axis: peer},
                device_id_type=MESH,
            )
            c.start()
            copies.append(c)
    local_copies = []
    for a, mode in enumerate(modes):
        c = pltpu.make_async_copy(
            ins[a].at[me] if mode == "a2a" else ins[a], outs[a].at[me], local_sem.at[a]
        )
        c.start()
        local_copies.append(c)
    if with_weight:
        c = pltpu.make_async_copy(w_in, w_out.at[z], wloc)
        c.start()
        local_copies.append(c)
        sibling = me + 1 - 2 * half
        forwards = []
        for k in range(1, n_shard):
            src = lax.rem(z + n_shard - k, n_shard)
            pltpu.make_async_remote_copy(
                src_ref=w_in.at[mine],
                dst_ref=w_out.at[src, mine],
                send_sem=wsend.at[k],
                recv_sem=wrecv.at[k],
                device_id={"shard": lax.rem(z + k, n_shard)},
                device_id_type=MESH,
            ).wait_recv()
            c = pltpu.make_async_remote_copy(
                src_ref=w_out.at[src, mine],
                dst_ref=w_out.at[src, mine],
                send_sem=fsend.at[k],
                recv_sem=frecv.at[k],
                device_id={"dp": sibling},
                device_id_type=MESH,
            )
            c.start()
            forwards.append(c)
        other = pl.ds(pl.multiple_of((1 - half) * half_rows, half_rows), half_rows)
        for k in range(1, n_shard):
            src = lax.rem(z + n_shard - k, n_shard)
            pltpu.make_async_remote_copy(
                src_ref=w_out.at[src, other],
                dst_ref=w_out.at[src, other],
                send_sem=fsend.at[k],
                recv_sem=frecv.at[k],
                device_id={"dp": sibling},
                device_id_type=MESH,
            ).wait_recv()
        for c in forwards:
            c.wait_send()
        for c in w_copies:
            c.wait_send()
    for a, mode in enumerate(modes):
        for k in range(1, n):
            src = lax.rem(me + n - k, n)
            pltpu.make_async_remote_copy(
                src_ref=ins[a].at[src] if mode == "a2a" else ins[a],
                dst_ref=outs[a].at[src],
                send_sem=send_sem.at[a, k],
                recv_sem=recv_sem.at[a, k],
                device_id={axis: src},
                device_id_type=MESH,
            ).wait_recv()
    for c in copies:
        c.wait_send()
    for c in local_copies:
        c.wait()


def exchange(axis, arrays, modes, collective_id, weight=None):
    n = lax.axis_size(axis)
    n_shard = lax.axis_size("shard")
    outs = []
    for array, mode in zip(arrays, modes):
        block = array.shape[1:] if mode == "a2a" else array.shape
        outs.append(jax.ShapeDtypeStruct((n,) + block, array.dtype))
    sems = [
        pltpu.SemaphoreType.DMA((len(modes), n)),
        pltpu.SemaphoreType.DMA((len(modes), n)),
        pltpu.SemaphoreType.DMA((len(modes),)),
    ]
    operands = list(arrays)
    if weight is not None:
        operands.append(weight)
        outs.append(jax.ShapeDtypeStruct((n_shard,) + weight.shape, weight.dtype))
        sems += [pltpu.SemaphoreType.DMA((n_shard,))] * 4 + [pltpu.SemaphoreType.DMA]
    hbm = pl.BlockSpec(memory_space=pl.ANY)
    moved = sum(math.prod(o.shape) * o.dtype.itemsize for o in outs)
    return pl.pallas_call(
        functools.partial(
            exchange_kernel, axis, n, tuple(modes), int(weight is not None), n_shard
        ),
        out_shape=outs,
        in_specs=[hbm] * len(operands),
        out_specs=[hbm] * len(outs),
        scratch_shapes=sems,
        compiler_params=pltpu.CompilerParams(collective_id=collective_id, has_side_effects=True),
        cost_estimate=pl.CostEstimate(flops=0, bytes_accessed=20 * moved, transcendentals=0),
    )(*operands)


def pack_kernel(pick_ref, q_ref, g_ref, w_ref, out_ref):
    width = q_ref.shape[1]
    out_ref[0, :, :width] = q_ref[...]
    out_ref[0, :, width:] = (w_ref[...] * g_ref[...].astype(F32)).astype(BF16)


def pack_rows(pick, queries, logp, weight_col, block_rows, dp_size):
    width = queries.shape[1]
    return pl.pallas_call(
        pack_kernel,
        out_shape=jax.ShapeDtypeStruct((dp_size, block_rows, 2 * width), BF16),
        grid_spec=pltpu.PrefetchScalarGridSpec(
            num_scalar_prefetch=1,
            grid=(dp_size,),
            in_specs=[
                pl.BlockSpec((block_rows, width), lambda d, p: (p[d], 0)),
                pl.BlockSpec((block_rows, width), lambda d, p: (p[d], 0)),
                pl.BlockSpec((block_rows, 1), lambda d, p: (p[d], 0)),
            ],
            out_specs=pl.BlockSpec((1, block_rows, 2 * width), lambda d, p: (d, 0, 0)),
        ),
        cost_estimate=pl.CostEstimate(
            flops=0, bytes_accessed=8 * dp_size * block_rows * width, transcendentals=0
        ),
    )(pick, queries, logp, weight_col)


def dot_nt(a, b):
    return lax.dot_general(a, b, (((1,), (1,)), ((), ())), preferred_element_type=F32)


def dot_tn(a, b):
    return lax.dot_general(a, b, (((0,), (0,)), ((), ())), preferred_element_type=F32)


def attend_kernel(windows, src_ref, row_ref, low_ref, starts_ref, x_ref, k_ref, v_ref, qg_ref, kv_ref, dk, dv):
    slot = pl.program_id(0)
    stream_len = dk.shape[0]
    block_rows = x_ref.shape[1]
    half = QH * HD
    scale = 1.0 / math.sqrt(HD)
    first_row = row_ref[slot]
    low = (low_ref[slot] // 128) * 128
    span = first_row + block_rows - low

    @pl.when(slot == 0)
    def _():
        dk[...] = jnp.zeros_like(dk)
        dv[...] = jnp.zeros_like(dv)

    m_rows = GROUPS * block_rows
    pos = first_row + lax.rem(lax.broadcasted_iota(jnp.int32, (m_rows, 1), 0), block_rows)
    seg_low = jnp.zeros_like(pos)
    for r in range(1, starts_ref.shape[0]):
        seg_low = jnp.where(pos >= starts_ref[r], starts_ref[r], seg_low)

    def body(width):
        start = pl.multiple_of(jnp.minimum(low, stream_len - width), 128)
        j = start + lax.broadcasted_iota(jnp.int32, (m_rows, width), 1)
        allowed = (j >= seg_low) & (j <= pos)
        rows = pl.ds(start, width)
        for h in range(KVH):
            cols = slice(h * HD, (h + 1) * HD)
            base = h * GROUPS * HD
            q = jnp.concatenate(
                [x_ref[0, :, base + g * HD : base + (g + 1) * HD] for g in range(GROUPS)], axis=0
            )
            og = jnp.concatenate(
                [
                    x_ref[0, :, half + base + g * HD : half + base + (g + 1) * HD]
                    for g in range(GROUPS)
                ],
                axis=0,
            )
            k = k_ref[rows, cols]
            v = v_ref[rows, cols]
            s = jnp.where(allowed, dot_nt(q, k) * scale, masked_score)
            e = jnp.exp(s - jnp.max(s, axis=1, keepdims=True))
            p = e * (1.0 / jnp.sum(e, axis=1, keepdims=True))
            pb = p.astype(BF16)
            dp = dot_nt(og, v)
            delta = jnp.sum(pb.astype(F32) * dp, axis=1, keepdims=True)
            ds = (p * (dp - delta)).astype(BF16)
            dq = (jnp.dot(ds, k, preferred_element_type=F32) * scale).astype(BF16)
            for g in range(GROUPS):
                qg_ref[:, base + g * HD : base + (g + 1) * HD] = dq[
                    g * block_rows : (g + 1) * block_rows
                ]
            dk[rows, cols] += dot_tn(ds, q)
            dv[rows, cols] += dot_tn(pb, og)

    before = 0
    for width in windows:
        last = width == windows[-1]
        fits = (span > before) if last else (span > before) & (span <= width)

        @pl.when(fits)
        def _(width=width):
            body(width)

        before = width

    @pl.when(slot == pl.num_programs(0) - 1)
    def _():
        kw = dk.shape[1]
        kv_ref[:, :kw] = (dk[...] * scale).astype(BF16)
        kv_ref[:, kw:] = dv[...].astype(BF16)


def attend(src, first_row, low, starts, incoming, keys, values):
    stream_len, kw = keys.shape
    slots = src.shape[0]
    block_rows = incoming.shape[1]
    windows = tuple(w for w in (128, 256, 384, 512, 640, 768) if w < stream_len) + (stream_len,)
    whole = lambda s, *_: (0, 0)
    return pl.pallas_call(
        functools.partial(attend_kernel, windows),
        out_shape=[
            jax.ShapeDtypeStruct((slots * block_rows, QH * HD), BF16),
            jax.ShapeDtypeStruct((stream_len, 2 * kw), BF16),
        ],
        grid_spec=pltpu.PrefetchScalarGridSpec(
            num_scalar_prefetch=4,
            grid=(slots,),
            in_specs=[
                pl.BlockSpec((1, block_rows, incoming.shape[2]), lambda s, a, *_: (a[s], 0, 0)),
                pl.BlockSpec((stream_len, kw), whole),
                pl.BlockSpec((stream_len, kw), whole),
            ],
            out_specs=[
                pl.BlockSpec((block_rows, QH * HD), lambda s, *_: (s, 0)),
                pl.BlockSpec((stream_len, 2 * kw), whole),
            ],
            scratch_shapes=[pltpu.VMEM((stream_len, kw), F32), pltpu.VMEM((stream_len, kw), F32)],
        ),
        compiler_params=pltpu.CompilerParams(vmem_limit_bytes=48 * 1024 * 1024),
        cost_estimate=pl.CostEstimate(
            flops=20_000_000_000, bytes_accessed=60_000_000, transcendentals=4_000_000
        ),
    )(src, first_row, low, starts, incoming, keys, values)


def local(
    hidden_in,
    norm_gain,
    key_weight,
    queries,
    logp_grad,
    values,
    advantages,
    log_ratio,
    resp_lengths,
    block_slots,
):
    row_count, width = hidden_in.shape[1:]
    dp_size = lax.axis_size("dp")
    n_shard = lax.axis_size("shard")
    stream_len = row_count * dp_size
    blocks_dev = block_slots.shape[1]
    block_rows = row_count // blocks_dev
    slice_w, key_width = key_weight.shape
    here = lax.axis_index("dp")
    z = lax.axis_index("shard")
    row_ids = here * row_count + jnp.arange(row_count, dtype=jnp.int32)
    lengths = resp_lengths[0]
    starts = jnp.cumsum(lengths) - lengths
    position = row_ids - segment_starts(lengths, row_ids)

    slot_list = block_slots[0]
    dest_dev = slot_list // blocks_dev
    block_ids = jnp.arange(blocks_dev, dtype=jnp.int32)
    dev_ids = jnp.arange(dp_size, dtype=jnp.int32)
    pick = jnp.sum(jnp.where(dest_dev[None, :] == dev_ids[:, None], block_ids[None, :], 0), axis=1)
    weight_tok = token_weight(advantages[0], log_ratio[0])
    outgoing = pack_rows(
        pick, queries[0], logp_grad[0], weight_tok[:, None], block_rows, dp_size
    )
    slot_tile = jnp.broadcast_to(slot_list[:, None], (blocks_dev, 128))
    incoming, table, all_values, full_weight = exchange(
        "dp", [outgoing, slot_tile, values[0]], ["a2a", "ag", "ag"], 1, weight=key_weight
    )
    full_weight = full_weight.reshape(width, key_width)

    pieces = []
    for k in range(n_shard):
        target = lax.rem(z + k, n_shard)
        piece = lax.dynamic_slice_in_dim(hidden_in[0], target * slice_w, slice_w, 1)
        if k:
            piece = lax.ppermute(piece, "shard", [(i, (i + k) % n_shard) for i in range(n_shard)])
        pieces.append(piece)

    x_float = hidden_in[0].astype(F32)
    inv_rms = lax.rsqrt(jnp.mean(x_float * x_float, axis=1, keepdims=True) + norm_eps)
    normed = x_float * inv_rms
    gain_f = norm_gain.astype(F32)
    normed_in = (normed * gain_f[None, :]).astype(BF16)
    raw_keys = jnp.dot(normed_in, full_weight, preferred_element_type=F32)
    cosine_table, sine_table = rope_tables(position, HD)
    key_rows = (
        rotate(raw_keys.reshape(row_count, KVH, HD), cosine_table, sine_table)
        .astype(BF16)
        .reshape(row_count, key_width)
    )
    (all_keys,) = exchange("dp", [key_rows], ["ag"], 2)

    slot_table = table[:, :, 0].reshape(-1)
    my_slots = here * blocks_dev + block_ids
    all_blocks = jnp.arange(slot_table.shape[0], dtype=jnp.int32)
    source_block = jnp.sum(
        jnp.where(slot_table[None, :] == my_slots[:, None], all_blocks[None, :], 0), axis=1
    )
    first_row = source_block * block_rows
    low = segment_starts(lengths, first_row)
    query_grad, kv_part = attend(
        source_block // blocks_dev,
        first_row,
        low,
        starts,
        incoming,
        all_keys.reshape(stream_len, key_width),
        all_values.reshape(stream_len, key_width),
    )
    (parts,) = exchange("dp", [kv_part.reshape(dp_size, row_count, 2 * key_width)], ["a2a"], 3)
    kv_sum = jnp.sum(parts.astype(F32), axis=0)
    value_grad = kv_sum[:, key_width:].astype(BF16)
    raw_grad = (
        rotate(kv_sum[:, :key_width].reshape(row_count, KVH, HD), cosine_table, -sine_table)
        .astype(BF16)
        .reshape(row_count, key_width)
    )
    inv_tile = jnp.broadcast_to(inv_rms, (row_count, 128))
    raw_all, inv_all = exchange("shard", [raw_grad, inv_tile], ["ag", "ag"], 4)

    normed_grad = dot_nt(raw_grad, full_weight).astype(BF16)
    grad_f = normed_grad.astype(F32)
    scaled = grad_f * gain_f[None, :]
    input_grad = (
        inv_rms * (scaled - normed * jnp.mean(scaled * normed, axis=1, keepdims=True))
    ).astype(BF16)

    gain_own = lax.dynamic_slice_in_dim(gain_f, z * slice_w, slice_w, 0)
    weight_grad = jnp.zeros((slice_w, key_width), F32)
    gain_grad = jnp.zeros((slice_w,), F32)
    for k in range(n_shard):
        source = lax.rem(z + n_shard - k, n_shard)
        raw_k = lax.dynamic_index_in_dim(raw_all, source, 0, keepdims=False)
        inv_k = lax.dynamic_index_in_dim(inv_all, source, 0, keepdims=False)[:, :1]
        normed_k = pieces[k].astype(F32) * inv_k
        in_k = (normed_k * gain_own[None, :]).astype(BF16)
        weight_grad += dot_tn(in_k, raw_k).astype(BF16).astype(F32)
        grad_k = dot_nt(raw_k, key_weight).astype(BF16).astype(F32)
        gain_grad += jnp.sum(grad_k * normed_k, axis=0).astype(BF16).astype(F32)
    return (
        input_grad[None],
        query_grad[None],
        value_grad[None],
        weight_grad[None],
        gain_grad[None],
    )


def solution(mesh):
    placed = (
        P("shard", "dp", None),
        P(),
        P("shard", None),
        P("shard", "dp", None),
        P("shard", "dp", None),
        P("shard", "dp", None),
        P("shard", "dp"),
        P("shard", "dp"),
        P("shard", None),
        P("shard", "dp"),
    )
    return jax.shard_map(
        local,
        mesh=mesh,
        in_specs=placed,
        out_specs=(
            P("shard", "dp", None),
            P("shard", "dp", None),
            P("shard", "dp", None),
            P("dp", "shard", None),
            P("dp", "shard"),
        ),
        check_vma=False,
    )
```

time: 550 us -> 290 us (0.53)
  waiting for transfers between devices: 306 us -> 0.01 us
  Pallas kernels: 0 us -> 218 us
  blocking collectives: 46 us -> 0 us
  matrix products: 76.9 us -> 32.2 us
  local copies, waits for them, and re-layouts: 58.7 us -> 23.6 us
  other arithmetic: 30.9 us -> 6.99 us
  between operations: 15.8 us -> 1.08 us
  loops' own time: 8.72 us -> 0 us
    pallas_call x0 -> x6, Pallas kernels: none -> 218 us  [the longest x4 190 us: exchange(): pl.pallas_call(functools.partial(exchange_kernel, axis, n, tuple(modes),...]
    reduce_scatter x2 -> x0, waiting for transfers between devices: 144 us -> none  [the longest x1 107 us: local(): lax.psum_scatter(weight_term.astype(jnp.bfloat16), 'shard', scatter_dimen...]
    all_gather x3 -> x0, waiting for transfers between devices: 125 us -> none  [the longest x1 109 us: local(): full_weight = lax.all_gather(key_weight, 'shard', axis=0, tiled=True)]
    unnamed x2 -> x0, blocking collectives: 46 us -> none
    dot_general x33 -> x10, matrix products: 76.9 us -> 32.2 us  [the longest x5 16.6 us: dot_nt(): lax.dot_general(a, b, (((1,), (1,)), ((), ())), preferred_element_type=F32)]
    unnamed x7 -> x0, waiting for transfers between devices: 36.9 us -> none
    unnamed x38 -> x24, local copies, waits for them, and re-layouts: 16.7 us -> 2.58 us
    reduce_or x12 -> x0, other arithmetic: 9.26 us -> none  [guarded(): return lax.cond(jnp.any(allowed), compute, keep_state, state)]
  transfers between devices with their start and end apart: 7 -> 3, of which waited for: 5 -> 0; matrix products, arithmetic and copies ran while one was open for 12% -> 16% of each run, Pallas kernels for 0% -> 75%
where the time goes in v1:
time: 290 us; the launch traced here: 289 us
  Pallas kernels  218 us (75%)
  matrix products  32.2 us (11%)
  local copies, waits for them, and re-layouts  23.6 us (8%)
  starting transfers between devices  7.86 us (3%)
  other arithmetic  6.99 us (2%)
    pallas_call x4, Pallas kernels, exchange(): pl.pallas_call(functools.partial(exchange_kernel, axis, n, tuple(modes),...  190 us
    pallas_call x1, Pallas kernels, attend(): pl.pallas_call(functools.partial(attend_kernel, windows), out_shape=[jax....  20.3 us
    dot_general x5, matrix products, dot_nt(): lax.dot_general(a, b, (((1,), (1,)), ((), ())), preferred_element_type=F32)  16.6 us
    dot_general x1, local copies, waits for them, and re-layouts, local(): raw_keys = jnp.dot(normed_in, full_weight, preferred_element_type=F32)  11.4 us
    dot_general x4, matrix products, dot_tn(): lax.dot_general(a, b, (((0,), (0,)), ((), ())), preferred_element_type=F32)  9.65 us
    ppermute x3, starting transfers between devices, local(): lax.ppermute(piece, 'shard', [(i, (i + k) % n_shard) for i in range(n_sha...  7.86 us
    pallas_call x1, Pallas kernels, pack_rows(): pl.pallas_call(pack_kernel, out_shape=jax.ShapeDtypeStruct((dp_size, bloc...  6.84 us
    dot_general x1, matrix products, local(): raw_keys = jnp.dot(normed_in, full_weight, preferred_element_type=F32)  5.87 us
  transfers between devices with their start and end apart: 3, of which 0 were waited for; matrix products, arithmetic and copies ran while one was open for 16% of the time, Pallas kernels for 75%

profile of v1, /device:TPU:0, one launch (start us, length us, event | category | flops | bytes accessed | tf_op | source)
XLA Modules:
  0.0 289.2 jit_solution(10916401447076367579)
XLA Ops:
  0.7 2.7 dynamic-slice_bitcast_fusion
  3.4 4.0 %collective-permute-start.1 = (bf16[128,2048]{1,0:T(8,128)(2,1)}, bf16[128,2048]{1,0:T(8,128)(2,1)}, u32[]{:S(2)}, u32[]{:S(2)}) collective-permute-start(bf16[128,2048]{1,0:T(8,128)(2,1)} %get-tuple-element.23), channel_id=1, source_target_pairs={{0,2},{1,3},{2,0},{3,1},{4,6},{5,7},{6,4},{7,5},{8,10},{9,11},{10,... | collective-permute-start | bytes 1572872 | tf_op jit(solution)/shard_map/ppermute | solution.py:394
  7.5 1.6 collective-permute-start
  9.0 2.2 collective-permute-start.2
  13.3 6.8 %shard_map.137.refs_0_ = bf16[8,16,8192]{2,1,0:T(8,128)(2,1)} custom-call(s32[8]{0:T(128)} %select_reduce_fusion.3.pick_ref, bf16[128,4096]{1,0:T(8,128)(2,1)} %bitcast.121, bf16[128,4096]{1,0:T(8,128)(2,1)} %bitcast.122, f32[128,1]{1,0:T(8,128)} %copy.30.w_ref), custom_call_target="tpu_custom_call" | custom-call | bytes 4194304 | tf_op jit(solution)/shard_map/pallas_call | solution.py:214
  20.8 105.7 %shard_map.138 = (bf16[8,16,8192]{2,1,0:T(8,128)(2,1)}, s32[8,8,128]{2,1,0:T(8,128)}, bf16[8,128,512]{2,1,0:T(8,128)(2,1)}, bf16[4,2048,512]{2,1,0:T(8,128)(2,1)}) custom-call(bf16[8,16,8192]{2,1,0:T(8,128)(2,1)} %shard_map.137.refs_0_, s32[8,128]{1,0:T(8,128)} %broadcast_in_dim.57.refs_1_, bf16[128,512]{1,0:T(8,128)(2,1)} %bitcast.125, ...), custom_call_target="tpu_custom_call" | custom-call | bytes 231342080 | tf_op jit(solution)/shard_map/pallas_call | solution.py:193
  128.0 11.4 %copy.31 = bf16[512,8192]{1,0:T(8,128)(2,1)} copy(bf16[512,8192]{0,1:T(8,128)(2,1)} %bitcast.116) | data formatting | bytes 16777216 | tf_op jit(solution)/shard_map/dot_general | solution.py:402
  139.8 5.9 %fusion.22 = f32[128,4,128]{0,2,1:T(8,128)S(1)} fusion(bf16[4,128,8192]{2,1,0:T(8,128)(2,1)} %bitcast.118, bf16[1,128,8192]{2,1,0:T(8,128)(2,1)S(1)} %copy-done.3, f32[8192]{0:T(1024)S(1)} %convert_element_type.231, f32[128]{0:T(128)S(1)} %add_rsqrt_fusion), kind=kOutput, calls=%fused_computation.35 | convolution fusion | flops 1077936128 | bytes 10781184 | tf_op jit(solution)/shard_map/dot_general | solution.py:402
  146.5 15.1 %shard_map.139 = bf16[8,128,512]{2,1,0:T(8,128)(2,1)} custom-call(bf16[128,512]{1,0:T(8,128)(2,1)} %copy.35.refs_0_), custom_call_target="tpu_custom_call" | custom-call | bytes 20971520 | tf_op jit(solution)/shard_map/pallas_call | solution.py:193
  162.9 20.3 %shard_map.140 = (bf16[128,4096]{1,0:T(8,128)(2,1)}, bf16[1024,1024]{1,0:T(8,128)(2,1)S(1)}) custom-call(s32[8]{0:T(128)S(1)} %get-tuple-element.36.src_ref, s32[8]{0:T(128)S(1)} %get-tuple-element.35.row_ref, s32[8]{0:T(128)S(1)} %select_reduce_fusion.1.low_ref, s32[8]{0:T(128)S(1)} %get-tuple-element.39.starts_ref, ...), custom_call_target="tpu_custom_call" | custom-call | flops 20000000000 | bytes 60000000 | tf_op jit(solution)/shard_map/pallas_call | solution.py:321
  183.1 1.3 copy-done
  184.4 26.5 %shard_map.141 = bf16[8,128,1024]{2,1,0:T(8,128)(2,1)} custom-call(bf16[8,128,1024]{2,1,0:T(8,128)(2,1)} %bitcast.113), custom_call_target="tpu_custom_call" | custom-call | bytes 41943040 | tf_op jit(solution)/shard_map/pallas_call | solution.py:193
  211.0 2.0 convert_reduce_fusion
  214.0 8.4 %fusion.6 = (f32[128]{0:T(128)S(1)}, f32[128,8192]{1,0:T(8,128)}) fusion(bf16[1,128,8192]{2,1,0:T(8,128)(2,1)S(1)} %copy-done.3, f32[128]{0:T(128)S(1)} %add_rsqrt_fusion, f32[8192]{0:T(1024)S(1)} %convert_element_type.231, bf16[128,512]{0,1:T(8,128)(2,1)S(1)} %bitcast.120, bf16[8192,512]{1,0:T(8,128)(2,1)} %bitcast.117), kind=kOutput, calls=%fused_computation.9 | convolution fusion | flops 1081081728 | bytes 14844928 | tf_op jit(solution)/shard_map/dot_general | solution.py:234
  223.1 43.1 %shard_map.142 = (bf16[4,128,512]{2,1,0:T(8,128)(2,1)}, f32[4,128,128]{2,1,0:T(8,128)}) custom-call(bf16[128,512]{1,0:T(8,128)(2,1)} %copy.36.refs_0_, f32[128,128]{1,0:T(8,128)} %broadcast_in_dim.64.refs_1_), custom_call_target="tpu_custom_call" | custom-call | bytes 15728640 | tf_op jit(solution)/shard_map/pallas_call | solution.py:193
  267.3 2.6 fusion.27
  270.0 1.7 convolution_convert_fusion.4
  271.7 2.3 fusion.24
  275.0 1.9 fusion.30
  276.9 1.9 fusion.29
  278.8 1.9 fusion.28
  281.3 1.8 convolution_convert_fusion.2
  283.1 1.9 convolution_convert_fusion.3
  285.0 4.2 %add_bitcast_fusion = f32[1,2048,512]{2,1,0:T(8,128)} fusion(bf16[2048,512]{1,0:T(8,128)(2,1)S(1)} %convolution_convert_fusion.2, bf16[2048,512]{1,0:T(8,128)(2,1)S(1)} %convolution_convert_fusion.3, bf16[2048,512]{1,0:T(8,128)(2,1)S(1)} %convolution_convert_fusion.4, bf16[128,2048]{1,0:T(8,128)(2,1)} %collective-permute-done.2, ...), kind=kOutput, calls=%fused_computation.16 | convolution fusion | flops 277872640 | bytes 11149828 | tf_op jit(solution)/shard_map/dot_general | solution.py:238
  (65 shorter events, 10.9 us)
Async XLA Ops:
  0.6 10.7 %copy-start.3 = (bf16[1,128,8192]{2,1,0:T(8,128)(2,1)S(1)}, bf16[1,128,8192]{2,1,0:T(8,128)(2,1)}, u32[]{:S(2)}) copy-start(bf16[1,128,8192]{2,1,0:T(8,128)(2,1)} %param.10) | copy-start | bytes 6291460
  0.6 11.2 %copy-start.7 = (bf16[8192]{0:T(1024)(128)(2,1)S(1)}, bf16[8192]{0:T(1024)(128)(2,1)}, u32[]{:S(2)}) copy-start(bf16[8192]{0:T(1024)(128)(2,1)} %param.11) | copy-start | bytes 49156
  0.7 11.2 %copy-start.8 = (s32[1,8]{1,0:T(1,128)S(1)}, s32[1,8]{1,0:T(1,128)}, u32[]{:S(2)}) copy-start(s32[1,8]{1,0:T(1,128)} %param.19) | copy-start | bytes 100
  0.7 11.9 %copy-start.10 = (f32[1,128]{1,0:T(1,128)S(1)}, f32[1,128]{1,0:T(1,128)}, u32[]{:S(2)}) copy-start(f32[1,128]{1,0:T(1,128)} %param.17) | copy-start | bytes 1540
  0.7 11.8 %copy-start.11 = (f32[1,128]{1,0:T(1,128)S(1)}, f32[1,128]{1,0:T(1,128)}, u32[]{:S(2)}) copy-start(f32[1,128]{1,0:T(1,128)} %param.16) | copy-start | bytes 1540
  3.4 273.5 %collective-permute-start.1 = (bf16[128,2048]{1,0:T(8,128)(2,1)}, bf16[128,2048]{1,0:T(8,128)(2,1)}, u32[]{:S(2)}, u32[]{:S(2)}) collective-permute-start(bf16[128,2048]{1,0:T(8,128)(2,1)} %get-tuple-element.23), channel_id=1, source_target_pairs={{0,2},{1,3},{2,0},{3,1},{4,6},{5,7},{6,4},{7,5},{8,10},{9,11},{10,... | collective-permute-start | bytes 1572872 | tf_op jit(solution)/shard_map/ppermute | solution.py:394
  7.5 271.3 %collective-permute-start = (bf16[128,2048]{1,0:T(8,128)(2,1)}, bf16[128,2048]{1,0:T(8,128)(2,1)}, u32[]{:S(2)}, u32[]{:S(2)}) collective-permute-start(bf16[128,2048]{1,0:T(8,128)(2,1)} %get-tuple-element.22), channel_id=1, source_target_pairs={{0,1},{1,2},{2,3},{3,0},{4,5},{5,6},{6,7},{7,4},{8,9},{9,10},{10,1... | collective-permute-start | bytes 1572872 | tf_op jit(solution)/shard_map/ppermute | solution.py:394
  9.0 266.0 %collective-permute-start.2 = (bf16[128,2048]{1,0:T(8,128)(2,1)}, bf16[128,2048]{1,0:T(8,128)(2,1)}, u32[]{:S(2)}, u32[]{:S(2)}) collective-permute-start(bf16[128,2048]{1,0:T(8,128)(2,1)} %get-tuple-element.21), channel_id=1, source_target_pairs={{0,3},{1,0},{2,1},{3,2},{4,7},{5,4},{6,5},{7,6},{8,11},{9,8},{10,9... | collective-permute-start | bytes 1572872 | tf_op jit(solution)/shard_map/ppermute | solution.py:394
  13.3 114.3 %copy-start.9 = (s32[1,8]{1,0:T(1,128)S(1)}, s32[1,8]{1,0:T(1,128)}, u32[]{:S(2)}) copy-start(s32[1,8]{1,0:T(1,128)} %param.18) | copy-start | bytes 100
  139.8 21.8 %copy-start.2 = (bf16[8,128,512]{2,1,0:T(8,128)(2,1)S(1)}, bf16[8,128,512]{2,1,0:T(8,128)(2,1)}, u32[]{:S(2)}) copy-start(bf16[8,128,512]{2,1,0:T(8,128)(2,1)} %get-tuple-element.16) | copy-start | bytes 3145732
  161.6 1.2 copy-start.1
  183.1 1.3 copy-start
  267.3 4.4 %copy-start.4 = (f32[128,8192]{1,0:T(8,128)S(1)}, f32[128,8192]{1,0:T(8,128)}, u32[]{:S(2)}) copy-start(f32[128,8192]{1,0:T(8,128)} %get-tuple-element.38) | copy-start | bytes 12582916
  271.7 3.3 %copy-start.5 = (bf16[2048,512]{1,0:T(8,128)(2,1)S(1)}, bf16[2048,512]{1,0:T(8,128)(2,1)}, u32[]{:S(2)}) copy-start(bf16[2048,512]{1,0:T(8,128)(2,1)} %refs_3_.1) | copy-start | bytes 6291460
  271.7 3.3 %copy-start.6 = (bf16[4,128,512]{2,1,0:T(8,128)(2,1)S(1)}, bf16[4,128,512]{2,1,0:T(8,128)(2,1)}, u32[]{:S(2)}) copy-start(bf16[4,128,512]{2,1,0:T(8,128)(2,1)} %get-tuple-element.20) | copy-start | bytes 1572868

commit v2 on v1

--- a/solution.py
+++ b/solution.py
@@ -28,15 +28,6 @@
     frequency = rope_base ** (-(jnp.arange(half_size, dtype=F32) * 2.0) / head_size)
     angles = positions.astype(F32)[:, None] * frequency[None, :]
     return (jnp.cos(angles)[:, None, :], jnp.sin(angles)[:, None, :])
-
-
-def rotate(tensor, cosine_table, sine_table):
-    half_size = tensor.shape[-1] // 2
-    a = tensor[..., :half_size]
-    b = tensor[..., half_size:]
-    return jnp.concatenate(
-        [a * cosine_table - b * sine_table, b * cosine_table + a * sine_table], axis=-1
-    )
 
 
 def segment_starts(lengths, row_ids):
@@ -75,14 +66,26 @@
 
     w_copies = []
     if with_weight:
-        wsend, wrecv, fsend, frecv, wloc = rest[3:]
+        wsend, wrecv, fsend, frecv, nsend, nrecv, gsend, grecv, wloc = rest[3:]
         w_in, w_out = ins[count], outs[count]
-        rows = w_in.shape[0]
-        half_rows = rows // 2
-        half = lax.rem(me, 2)
-        mine = pl.ds(pl.multiple_of(half * half_rows, half_rows), half_rows)
-        for k in range(1, n_shard):
-            c = pltpu.make_async_remote_copy(
+        part_rows = w_in.shape[0] // 4
+        core = lax.rem(me, 2)
+        bit1 = lax.rem(lax.div(me, 2), 2)
+        bit2 = lax.rem(lax.div(me, 4), 2)
+        color = lax.rem(bit1 + bit2, 2)
+        sibling = me + 1 - 2 * core
+        neighbour = me + (1 - core) * (2 - 4 * bit1) + core * (4 - 8 * bit2)
+
+        def part(index):
+            return pl.ds(pl.multiple_of(index * part_rows, part_rows), part_rows)
+
+        mine = part(2 * color + core)
+        theirs = part(2 * (1 - color) + core)
+        sib_mine = part(2 * color + 1 - core)
+        sib_theirs = part(2 * (1 - color) + 1 - core)
+
+        def over_z(k):
+            return pltpu.make_async_remote_copy(
                 src_ref=w_in.at[mine],
                 dst_ref=w_out.at[z, mine],
                 send_sem=wsend.at[k],
@@ -90,6 +93,19 @@
                 device_id={"shard": lax.rem(z + k, n_shard)},
                 device_id_type=MESH,
             )
+
+        def hand_on(source, rows, send, recv, k, target):
+            return pltpu.make_async_remote_copy(
+                src_ref=w_out.at[source, rows],
+                dst_ref=w_out.at[source, rows],
+                send_sem=send.at[k],
+                recv_sem=recv.at[k],
+                device_id={"dp": target},
+                device_id_type=MESH,
+            )
+
+        for k in range(1, n_shard):
+            c = over_z(k)
             c.start()
             w_copies.append(c)
     copies = []
@@ -117,41 +133,30 @@
         c = pltpu.make_async_copy(w_in, w_out.at[z], wloc)
         c.start()
         local_copies.append(c)
-        sibling = me + 1 - 2 * half
-        forwards = []
+        sources = [lax.rem(z + n_shard - k, n_shard) for k in range(n_shard)]
         for k in range(1, n_shard):
-            src = lax.rem(z + n_shard - k, n_shard)
             pltpu.make_async_remote_copy(
                 src_ref=w_in.at[mine],
-                dst_ref=w_out.at[src, mine],
+                dst_ref=w_out.at[sources[k], mine],
                 send_sem=wsend.at[k],
                 recv_sem=wrecv.at[k],
                 device_id={"shard": lax.rem(z + k, n_shard)},
                 device_id_type=MESH,
             ).wait_recv()
-            c = pltpu.make_async_remote_copy(
-                src_ref=w_out.at[src, mine],
-                dst_ref=w_out.at[src, mine],
-                send_sem=fsend.at[k],
-                recv_sem=frecv.at[k],
-                device_id={"dp": sibling},
-                device_id_type=MESH,
-            )
+            for c in (
+                hand_on(sources[k], mine, nsend, nrecv, k, neighbour),
+                hand_on(sources[k], mine, fsend, frecv, k, sibling),
+            ):
+                c.start()
+                w_copies.append(c)
+        for k in range(1, n_shard):
+            hand_on(sources[k], theirs, nsend, nrecv, k, neighbour).wait_recv()
+            c = hand_on(sources[k], theirs, gsend, grecv, k, sibling)
             c.start()
-            forwards.append(c)
-        other = pl.ds(pl.multiple_of((1 - half) * half_rows, half_rows), half_rows)
+            w_copies.append(c)
         for k in range(1, n_shard):
-            src = lax.rem(z + n_shard - k, n_shard)
-            pltpu.make_async_remote_copy(
-                src_ref=w_out.at[src, other],
-                dst_ref=w_out.at[src, other],
-                send_sem=fsend.at[k],
-                recv_sem=frecv.at[k],
-                device_id={"dp": sibling},
-                device_id_type=MESH,
-            ).wait_recv()
-        for c in forwards:
-            c.wait_send()
+            hand_on(sources[k], sib_mine, fsend, frecv, k, sibling).wait_recv()
+            hand_on(sources[k], sib_theirs, gsend, grecv, k, sibling).wait_recv()
         for c in w_copies:
             c.wait_send()
     for a, mode in enumerate(modes):
@@ -187,7 +192,7 @@
     if weight is not None:
         operands.append(weight)
         outs.append(jax.ShapeDtypeStruct((n_shard,) + weight.shape, weight.dtype))
-        sems += [pltpu.SemaphoreType.DMA((n_shard,))] * 4 + [pltpu.SemaphoreType.DMA]
+        sems += [pltpu.SemaphoreType.DMA((n_shard,))] * 8 + [pltpu.SemaphoreType.DMA]
     hbm = pl.BlockSpec(memory_space=pl.ANY)
     moved = sum(math.prod(o.shape) * o.dtype.itemsize for o in outs)
     return pl.pallas_call(
@@ -345,6 +350,198 @@
     )(src, first_row, low, starts, incoming, keys, values)
 
 
+def keys_kernel(x_ref, w_ref, gain_ref, cos_ref, sin_ref, key_ref, inv_ref, acc, inv):
+    step = pl.program_id(0)
+    chunk = w_ref.shape[0]
+    width = x_ref.shape[1]
+
+    @pl.when(step == 0)
+    def _():
+        total = jnp.zeros((x_ref.shape[0], 1), F32)
+        for c in range(0, width, 1024):
+            x = x_ref[:, c : c + 1024].astype(F32)
+            total += jnp.sum(x * x, axis=1, keepdims=True)
+        inv[...] = lax.rsqrt(total / width + norm_eps)
+        inv_ref[...] = jnp.broadcast_to(inv[...], inv_ref.shape)
+        acc[...] = jnp.zeros_like(acc)
+
+    cols = pl.ds(pl.multiple_of(step * chunk, chunk), chunk)
+    normed = x_ref[:, cols].astype(F32) * inv[...]
+    normed_in = (normed * gain_ref[:, cols].astype(F32)).astype(BF16)
+    acc[...] += jnp.dot(normed_in, w_ref[...], preferred_element_type=F32)
+
+    @pl.when(step == pl.num_programs(0) - 1)
+    def _():
+        half = HD // 2
+        cos, sin = cos_ref[...], sin_ref[...]
+        for h in range(KVH):
+            a = acc[:, h * HD : h * HD + half]
+            b = acc[:, h * HD + half : (h + 1) * HD]
+            key_ref[:, h * HD : (h + 1) * HD] = jnp.concatenate(
+                [a * cos - b * sin, b * cos + a * sin], axis=1
+            ).astype(BF16)
+
+
+def make_keys(x, weight, gain, cos, sin):
+    rows, width = x.shape
+    kw = weight.shape[1]
+    chunk = 1024
+    whole = lambda c: (0, 0)
+    return pl.pallas_call(
+        keys_kernel,
+        out_shape=[
+            jax.ShapeDtypeStruct((rows, kw), BF16),
+            jax.ShapeDtypeStruct((rows, 128), F32),
+        ],
+        grid=(width // chunk,),
+        in_specs=[
+            pl.BlockSpec((rows, width), whole),
+            pl.BlockSpec((chunk, kw), lambda c: (c, 0)),
+            pl.BlockSpec((1, width), whole),
+            pl.BlockSpec(cos.shape, whole),
+            pl.BlockSpec(sin.shape, whole),
+        ],
+        out_specs=[pl.BlockSpec((rows, kw), whole), pl.BlockSpec((rows, 128), whole)],
+        scratch_shapes=[pltpu.VMEM((rows, kw), F32), pltpu.VMEM((rows, 1), F32)],
+        compiler_params=pltpu.CompilerParams(vmem_limit_bytes=40 * 1024 * 1024),
+        cost_estimate=pl.CostEstimate(
+            flops=2 * rows * width * kw, bytes_accessed=4 * width * kw, transcendentals=0
+        ),
+    )(x, weight, gain, cos, sin)
+
+
+def raw_kernel(parts_ref, cos_ref, sin_ref, raw_ref, value_ref):
+    kw = raw_ref.shape[1]
+    half = HD // 2
+    total = parts_ref[0].astype(F32)
+    for i in range(1, parts_ref.shape[0]):
+        total += parts_ref[i].astype(F32)
+    value_ref[...] = total[:, kw:].astype(BF16)
+    cos, sin = cos_ref[...], sin_ref[...]
+    for h in range(KVH):
+        a = total[:, h * HD : h * HD + half]
+        b = total[:, h * HD + half : (h + 1) * HD]
+        raw_ref[:, h * HD : (h + 1) * HD] = jnp.concatenate(
+            [a * cos + b * sin, b * cos - a * sin], axis=1
+        ).astype(BF16)
+
+
+def make_raw(parts, cos, sin):
+    rows = parts.shape[1]
+    kw = parts.shape[2] // 2
+    return pl.pallas_call(
+        raw_kernel,
+        out_shape=[jax.ShapeDtypeStruct((rows, kw), BF16)] * 2,
+        compiler_params=pltpu.CompilerParams(vmem_limit_bytes=40 * 1024 * 1024),
+    )(parts, cos, sin)
+
+
+def rows_kernel(raw_ref, w_ref, x_ref, inv_ref, gain_ref, out_ref, grads, total):
+    step = pl.program_id(0)
+    chunk = w_ref.shape[0]
+    width = x_ref.shape[1]
+    inv = inv_ref[:, :1]
+
+    @pl.when(step == 0)
+    def _():
+        total[...] = jnp.zeros_like(total)
+
+    cols = pl.ds(pl.multiple_of(step * chunk, chunk), chunk)
+    grad = dot_nt(raw_ref[...], w_ref[...]).astype(BF16)
+    grads[:, cols] = grad
+    scaled = grad.astype(F32) * gain_ref[:, cols].astype(F32)
+    normed = x_ref[:, cols].astype(F32) * inv
+    total[...] += jnp.sum(scaled * normed, axis=1, keepdims=True)
+
+    @pl.when(step == pl.num_programs(0) - 1)
+    def _():
+        mean = total[...] / width
+        for c in range(0, width, 1024):
+            part = slice(c, c + 1024)
+            scaled = grads[:, part].astype(F32) * gain_ref[:, part].astype(F32)
+            normed = x_ref[:, part].astype(F32) * inv
+            out_ref[:, part] = (inv * (scaled - normed * mean)).astype(BF16)
+
+
+def own_rows(raw, weight, x, inv, gain):
+    rows, width = x.shape
+    kw = weight.shape[1]
+    chunk = 1024
+    whole = lambda c: (0, 0)
+    return pl.pallas_call(
+        rows_kernel,
+        out_shape=jax.ShapeDtypeStruct((rows, width), BF16),
+        grid=(width // chunk,),
+        in_specs=[
+            pl.BlockSpec((rows, kw), whole),
+            pl.BlockSpec((chunk, kw), lambda c: (c, 0)),
+            pl.BlockSpec((rows, width), whole),
+            pl.BlockSpec((rows, 128), whole),
+            pl.BlockSpec((1, width), whole),
+        ],
+        out_specs=pl.BlockSpec((rows, width), whole),
+        scratch_shapes=[pltpu.VMEM((rows, width), BF16), pltpu.VMEM((rows, 1), F32)],
+        compiler_params=pltpu.CompilerParams(vmem_limit_bytes=40 * 1024 * 1024),
+        cost_estimate=pl.CostEstimate(
+            flops=2 * rows * width * kw, bytes_accessed=4 * width * kw, transcendentals=0
+        ),
+    )(raw, weight, x, inv, gain)
+
+
+def own_kernel(n, z_ref, raw_ref, inv_ref, w_ref, gain_ref, *refs):
+    pieces, (wg_ref, gg_ref) = refs[:n], refs[n:]
+    z = z_ref[0]
+    gain = gain_ref[...].astype(F32)
+    weight = w_ref[...]
+    weight_sum = None
+    for k in range(n):
+        source = lax.rem(z + n - k, n)
+        raw = raw_ref[source]
+        inv = inv_ref[source][:, :1]
+        normed = pieces[k][...].astype(F32) * inv
+        term = dot_tn((normed * gain).astype(BF16), raw).astype(BF16).astype(F32)
+        grad = dot_nt(raw, weight).astype(BF16).astype(F32)
+        row = jnp.sum(grad * normed, axis=0, keepdims=True).astype(BF16).astype(F32)
+        weight_sum = term if k == 0 else weight_sum + term
+        gain_sum = row if k == 0 else gain_sum + row
+    wg_ref[...] = weight_sum
+    gg_ref[...] = gain_sum
+
+
+def own_weight(z, raw_all, inv_all, weight, gain, pieces):
+    n, rows, kw = raw_all.shape
+    slice_w = weight.shape[0]
+    chunk = min(256, slice_w)
+    steps = slice_w // chunk
+    whole = lambda c, zr: (0, 0, 0)
+    return pl.pallas_call(
+        functools.partial(own_kernel, n),
+        out_shape=[
+            jax.ShapeDtypeStruct((slice_w, kw), F32),
+            jax.ShapeDtypeStruct((1, slice_w), F32),
+        ],
+        grid_spec=pltpu.PrefetchScalarGridSpec(
+            num_scalar_prefetch=1,
+            grid=(steps,),
+            in_specs=[
+                pl.BlockSpec(raw_all.shape, whole),
+                pl.BlockSpec(inv_all.shape, whole),
+                pl.BlockSpec((chunk, kw), lambda c, zr: (c, 0)),
+                pl.BlockSpec((1, chunk), lambda c, zr: (0, zr[0] * steps + c)),
+            ]
+            + [pl.BlockSpec((rows, chunk), lambda c, zr: (0, c))] * n,
+            out_specs=[
+                pl.BlockSpec((chunk, kw), lambda c, zr: (c, 0)),
+                pl.BlockSpec((1, chunk), lambda c, zr: (0, c)),
+            ],
+        ),
+        compiler_params=pltpu.CompilerParams(vmem_limit_bytes=40 * 1024 * 1024),
+        cost_estimate=pl.CostEstimate(
+            flops=4 * n * rows * slice_w * kw, bytes_accessed=12 * slice_w * kw, transcendentals=0
+        ),
+    )(z.reshape(1), raw_all, inv_all, weight, gain, *pieces)
+
+
 def local(
     hidden_in,
     norm_gain,
@@ -389,23 +586,16 @@
     pieces = []
     for k in range(n_shard):
         target = lax.rem(z + k, n_shard)
-        piece = lax.dynamic_slice_in_dim(hidden_in[0], target * slice_w, slice_w, 1)
-        if k:
-            piece = lax.ppermute(piece, "shard", [(i, (i + k) % n_shard) for i in range(n_shard)])
-        pieces.append(piece)
-
-    x_float = hidden_in[0].astype(F32)
-    inv_rms = lax.rsqrt(jnp.mean(x_float * x_float, axis=1, keepdims=True) + norm_eps)
-    normed = x_float * inv_rms
-    gain_f = norm_gain.astype(F32)
-    normed_in = (normed * gain_f[None, :]).astype(BF16)
-    raw_keys = jnp.dot(normed_in, full_weight, preferred_element_type=F32)
-    cosine_table, sine_table = rope_tables(position, HD)
-    key_rows = (
-        rotate(raw_keys.reshape(row_count, KVH, HD), cosine_table, sine_table)
-        .astype(BF16)
-        .reshape(row_count, key_width)
-    )
+        pieces.append(lax.dynamic_slice_in_dim(hidden_in[0], target * slice_w, slice_w, 1))
+    pieces, full_weight = lax.optimization_barrier((pieces, full_weight))
+    for k in range(1, n_shard):
+        pieces[k] = lax.ppermute(
+            pieces[k], "shard", [(i, (i + k) % n_shard) for i in range(n_shard)]
+        )
+
+    gain_row = norm_gain[None, :]
+    cos, sin = (t[:, 0, :] for t in rope_tables(position, HD))
+    key_rows, inv_tile = make_keys(hidden_in[0], full_weight, gain_row, cos, sin)
     (all_keys,) = exchange("dp", [key_rows], ["ag"], 2)
 
     slot_table = table[:, :, 0].reshape(-1)
@@ -426,41 +616,16 @@
         all_values.reshape(stream_len, key_width),
     )
     (parts,) = exchange("dp", [kv_part.reshape(dp_size, row_count, 2 * key_width)], ["a2a"], 3)
-    kv_sum = jnp.sum(parts.astype(F32), axis=0)
-    value_grad = kv_sum[:, key_width:].astype(BF16)
-    raw_grad = (
-        rotate(kv_sum[:, :key_width].reshape(row_count, KVH, HD), cosine_table, -sine_table)
-        .astype(BF16)
-        .reshape(row_count, key_width)
-    )
-    inv_tile = jnp.broadcast_to(inv_rms, (row_count, 128))
+    raw_grad, value_grad = make_raw(parts, cos, sin)
     raw_all, inv_all = exchange("shard", [raw_grad, inv_tile], ["ag", "ag"], 4)
-
-    normed_grad = dot_nt(raw_grad, full_weight).astype(BF16)
-    grad_f = normed_grad.astype(F32)
-    scaled = grad_f * gain_f[None, :]
-    input_grad = (
-        inv_rms * (scaled - normed * jnp.mean(scaled * normed, axis=1, keepdims=True))
-    ).astype(BF16)
-
-    gain_own = lax.dynamic_slice_in_dim(gain_f, z * slice_w, slice_w, 0)
-    weight_grad = jnp.zeros((slice_w, key_width), F32)
-    gain_grad = jnp.zeros((slice_w,), F32)
-    for k in range(n_shard):
-        source = lax.rem(z + n_shard - k, n_shard)
-        raw_k = lax.dynamic_index_in_dim(raw_all, source, 0, keepdims=False)
-        inv_k = lax.dynamic_index_in_dim(inv_all, source, 0, keepdims=False)[:, :1]
-        normed_k = pieces[k].astype(F32) * inv_k
-        in_k = (normed_k * gain_own[None, :]).astype(BF16)
-        weight_grad += dot_tn(in_k, raw_k).astype(BF16).astype(F32)
-        grad_k = dot_nt(raw_k, key_weight).astype(BF16).astype(F32)
-        gain_grad += jnp.sum(grad_k * normed_k, axis=0).astype(BF16).astype(F32)
+    input_grad = own_rows(raw_grad, full_weight, hidden_in[0], inv_tile, gain_row)
+    weight_grad, gain_grad = own_weight(z, raw_all, inv_all, key_weight, gain_row, pieces)
     return (
         input_grad[None],
         query_grad[None],
         value_grad[None],
         weight_grad[None],
-        gain_grad[None],
+        gain_grad,
     )
 
 

time: 290 us -> 220 us (0.76)
  matrix products: 32.2 us -> 0 us
  Pallas kernels: 218 us -> 192 us
  local copies, waits for them, and re-layouts: 23.6 us -> 17.9 us
  other arithmetic: 6.99 us -> 2.96 us
  starting transfers between devices: 7.86 us -> 4.36 us
    pallas_call x4, Pallas kernels: 190 us -> 142 us  [exchange(): pl.pallas_call(functools.partial(exchange_kernel, axis, n, tuple(modes),...]
    dot_general x10 -> x0, matrix products: 32.2 us -> none  [the longest x5 16.6 us: dot_nt(): lax.dot_general(a, b, (((1,), (1,)), ((), ())), preferred_element_type=F32)]
    pallas_call x0 -> x4, Pallas kernels: none -> 21.6 us  [the longest x1 9.1 us: own_weight(): pl.pallas_call(functools.partial(own_kernel, n), out_shape=[jax.ShapeDtyp...]
    unnamed x24 -> x38, local copies, waits for them, and re-layouts: 2.58 us -> 15 us
    dot_general x1 -> x0, local copies, waits for them, and re-layouts: 11.4 us -> none  [local(): raw_keys = jnp.dot(normed_in, full_weight, preferred_element_type=F32)]
    ppermute x3, starting transfers between devices: 7.86 us -> 4.36 us  [local(): lax.ppermute(pieces[k], 'shard', [(i, (i + k) % n_shard) for i in range(n...]
  transfers between devices with their start and end apart: 3 -> 3, of which waited for: 0 -> 0; matrix products, arithmetic and copies ran while one was open for 16% -> 1% of each run, Pallas kernels for 75% -> 43%
where the time goes in v2:
time: 220 us; the launch traced here: 218 us
  Pallas kernels  192 us (87%)
  local copies, waits for them, and re-layouts  17.9 us (8%)
  starting transfers between devices  4.36 us (2%)
  other arithmetic  2.96 us (1%)
    pallas_call x4, Pallas kernels, exchange(): pl.pallas_call(functools.partial(exchange_kernel, axis, n, tuple(modes),...  142 us
    pallas_call x1, Pallas kernels, attend(): pl.pallas_call(functools.partial(attend_kernel, windows), out_shape=[jax....  21.1 us
    unnamed x38, local copies, waits for them, and re-layouts  15 us
    pallas_call x1, Pallas kernels, own_weight(): pl.pallas_call(functools.partial(own_kernel, n), out_shape=[jax.ShapeDtyp...  9.1 us
    pallas_call x1, Pallas kernels, own_rows(): pl.pallas_call(rows_kernel, out_shape=jax.ShapeDtypeStruct((rows, width),...  7.63 us
    pallas_call x1, Pallas kernels, pack_rows(): pl.pallas_call(pack_kernel, out_shape=jax.ShapeDtypeStruct((dp_size, bloc...  6.84 us
  transfers between devices with their start and end apart: 3, of which 0 were waited for; matrix products, arithmetic and copies ran while one was open for 1% of the time, Pallas kernels for 43%

profile of v2, /device:TPU:0, one launch (start us, length us, event | category | flops | bytes accessed | tf_op | source)
XLA Modules:
  0.0 217.8 jit_solution(10442713791387071375)
XLA Ops:
  0.7 0.7 fusion.1
  1.9 0.7 fusion.2
  2.6 0.7 copy.17.w_ref
  3.4 6.8 %shard_map.137.refs_0_ = bf16[8,16,8192]{2,1,0:T(8,128)(2,1)} custom-call(s32[8]{0:T(128)} %select_reduce_fusion.3.pick_ref, bf16[128,4096]{1,0:T(8,128)(2,1)} %bitcast.45, bf16[128,4096]{1,0:T(8,128)(2,1)} %bitcast.46, f32[128,1]{1,0:T(8,128)} %copy.17.w_ref), custom_call_target="tpu_custom_call" | custom-call | bytes 4194304 | tf_op jit(solution)/shard_map/pallas_call | solution.py:219
  10.2 0.7 broadcast_in_dim.83.refs_1_
  10.9 82.5 %shard_map.138 = (bf16[8,16,8192]{2,1,0:T(8,128)(2,1)}, s32[8,8,128]{2,1,0:T(8,128)}, bf16[8,128,512]{2,1,0:T(8,128)(2,1)}, bf16[4,2048,512]{2,1,0:T(8,128)(2,1)}) custom-call(bf16[8,16,8192]{2,1,0:T(8,128)(2,1)} %shard_map.137.refs_0_, s32[8,128]{1,0:T(8,128)} %broadcast_in_dim.83.refs_1_, bf16[128,512]{1,0:T(8,128)(2,1)} %bitcast.47, bf16[2048,512]{1,0:T(8,128)(2,1)} %w_ref.1), custom_call_target="tpu_custom_call" | custom-call | bytes 231342080 | tf_op jit(solution)/shard_map/pallas_call | solution.py:198
  93.5 1.2 dynamic-slice_bitcast_fusion
  95.2 2.4 %collective-permute-start.1 = (bf16[128,2048]{1,0:T(8,128)(2,1)}, bf16[128,2048]{1,0:T(8,128)(2,1)}, u32[]{:S(2)}, u32[]{:S(2)}) collective-permute-start(bf16[128,2048]{1,0:T(8,128)(2,1)} %get-tuple-element.39), channel_id=1, source_target_pairs={{0,2},{1,3},{2,0},{3,1},{4,6},{5,7},{6,4},{7,5},{8,10},{9,11},{10,... | collective-permute-start | bytes 1572872 | tf_op jit(solution)/shard_map/ppermute | solution.py:592
  97.6 1.3 collective-permute-start.2
  100.3 3.4 %copy-done = bf16[4,2048,512]{2,1,0:T(8,128)(2,1)S(1)} copy-done((bf16[4,2048,512]{2,1,0:T(8,128)(2,1)S(1)}, bf16[4,2048,512]{2,1,0:T(8,128)(2,1)}, u32[]{:S(2)}) %copy-start) | copy-done | bytes 8388632
  103.7 3.8 %shard_map.139 = (bf16[128,512]{1,0:T(8,128)(2,1)S(1)}, f32[128,128]{1,0:T(8,128)S(1)}) custom-call(bf16[128,8192]{1,0:T(8,128)(2,1)S(1)} %bitcast.39, bf16[8192,512]{1,0:T(8,128)(2,1)S(1)} %bitcast.37, bf16[1,8192]{1,0:T(2,128)(2,1)S(1)} %broadcast_in_dim.86.gain_ref, f32[128,64]{1,0:T(8,128)S(1)} %get-tuple-element.48.cos_ref, ...), custom_call_target="tpu_custom_call" | custom-call | flops 1073741824 | bytes 16777216 | tf_op jit(solution)/shard_map/pallas_call | solution.py:390
  108.8 14.2 %shard_map.140 = bf16[8,128,512]{2,1,0:T(8,128)(2,1)} custom-call(bf16[128,512]{1,0:T(8,128)(2,1)} %copy-done.11), custom_call_target="tpu_custom_call" | custom-call | bytes 20971520 | tf_op jit(solution)/shard_map/pallas_call | solution.py:198
  123.0 1.2 copy-done.6
  124.2 1.2 copy-done.12
  125.4 21.1 %shard_map.141 = (bf16[128,4096]{1,0:T(8,128)(2,1)}, bf16[1024,1024]{1,0:T(8,128)(2,1)S(1)}) custom-call(s32[8]{0:T(128)S(1)} %get-tuple-element.50.src_ref, s32[8]{0:T(128)S(1)} %get-tuple-element.49.row_ref, s32[8]{0:T(128)S(1)} %select_reduce_fusion.1.low_ref, s32[8]{0:T(128)S(1)} %get-tuple-element.51.starts_ref, ...), custom_call_target="tpu_custom_call" | custom-call | flops 20000000000 | bytes 60000000 | tf_op jit(solution)/shard_map/pallas_call | solution.py:326
  146.5 1.3 copy-done.5
  147.8 25.8 %shard_map.142.parts_ref = bf16[8,128,1024]{2,1,0:T(8,128)(2,1)} custom-call(bf16[8,128,1024]{2,1,0:T(8,128)(2,1)} %bitcast.41), custom_call_target="tpu_custom_call" | custom-call | bytes 41943040 | tf_op jit(solution)/shard_map/pallas_call | solution.py:198
  173.7 1.6 copy-done.3
  175.3 1.1 shard_map.143
  177.0 19.7 %shard_map.145 = (bf16[4,128,512]{2,1,0:T(8,128)(2,1)}, f32[4,128,128]{2,1,0:T(8,128)}) custom-call(bf16[128,512]{1,0:T(8,128)(2,1)} %copy-done.7, f32[128,128]{1,0:T(8,128)} %copy-done.9), custom_call_target="tpu_custom_call" | custom-call | bytes 15728640 | tf_op jit(solution)/shard_map/pallas_call | solution.py:198
  196.8 3.4 %copy-done.1 = bf16[4,2048,512]{2,1,0:T(8,128)(2,1)S(1)} copy-done((bf16[4,2048,512]{2,1,0:T(8,128)(2,1)S(1)}, bf16[4,2048,512]{2,1,0:T(8,128)(2,1)}, u32[]{:S(2)}) %copy-start.1) | copy-done | bytes 8388632
  200.2 0.9 copy-done.8
  201.1 7.6 %shard_map.144 = bf16[128,8192]{1,0:T(8,128)(2,1)} custom-call(bf16[128,512]{1,0:T(8,128)(2,1)S(1)} %copy-done.8, bf16[8192,512]{1,0:T(8,128)(2,1)S(1)} %bitcast.38, bf16[128,8192]{1,0:T(8,128)(2,1)S(1)} %bitcast.40, f32[128,128]{1,0:T(8,128)S(1)} %copy-done.10, bf16[1,8192]{1,0:T(2,128)(2,1)S(1)} %broadcast_in_dim.86.gain_ref), custom_call_target="tpu_custom_call" | custom-call | flops 1073741824 | bytes 16777216 | tf_op jit(solution)/shard_map/pallas_call | solution.py:471
  208.7 9.1 %shard_map.146 = (f32[2048,512]{1,0:T(8,128)}, f32[1,2048]{1,0:T(1,128)}) custom-call(s32[1]{0:T(128)} %bitcast.23.z_ref, bf16[4,128,512]{2,1,0:T(8,128)(2,1)S(1)} %copy-done.13, f32[4,128,128]{2,1,0:T(8,128)S(1)} %copy-done.14, bf16[2048,512]{1,0:T(8,128)(2,1)S(1)} %copy-done.4, bf16[1,8192]{1,0:T(2,128)(2,1)S(1)} %broadcast_in_dim.86.gain_ref, ...), custom_call_target="tpu_custom_call" | custom-call | flops 2147483648 | bytes 12582912 | tf_op jit(solution)/shard_map/pallas_call | solution.py:517
  (50 shorter events, 4.5 us)
Async XLA Ops:
  3.4 6.8 %copy-start.17 = (s32[1,8]{1,0:T(1,128)S(1)}, s32[1,8]{1,0:T(1,128)}, u32[]{:S(2)}) copy-start(s32[1,8]{1,0:T(1,128)} %param.19) | copy-start | bytes 100
  10.9 82.5 %copy-start.2 = (bf16[1,128,8192]{2,1,0:T(8,128)(2,1)S(1)}, bf16[1,128,8192]{2,1,0:T(8,128)(2,1)}, u32[]{:S(2)}) copy-start(bf16[1,128,8192]{2,1,0:T(8,128)(2,1)} %param.10) | copy-start | bytes 6291460
  93.4 5.6 %copy-start.18 = (s32[1,8]{1,0:T(1,128)S(1)}, s32[1,8]{1,0:T(1,128)}, u32[]{:S(2)}) copy-start(s32[1,8]{1,0:T(1,128)} %param.18) | copy-start | bytes 100
  93.4 5.9 %copy-start.16 = (bf16[8192]{0:T(1024)(128)(2,1)S(1)}, bf16[8192]{0:T(1024)(128)(2,1)}, u32[]{:S(2)}) copy-start(bf16[8192]{0:T(1024)(128)(2,1)} %param.11) | copy-start | bytes 49156
  93.4 5.9 %copy-start.15 = (s32[8,8,128]{2,1,0:T(8,128)S(1)}, s32[8,8,128]{2,1,0:T(8,128)}, u32[]{:S(2)}) copy-start(s32[8,8,128]{2,1,0:T(8,128)} %get-tuple-element.24) | copy-start | bytes 98308
  94.6 114.1 %collective-permute-start = (bf16[128,2048]{1,0:T(8,128)(2,1)}, bf16[128,2048]{1,0:T(8,128)(2,1)S(1)}, u32[]{:S(2)}, u32[]{:S(2)}) collective-permute-start(bf16[128,2048]{1,0:T(8,128)(2,1)} %get-tuple-element.38), channel_id=1, source_target_pairs={{0,1},{1,2},{2,3},{3,0},{4,5},{5,6},{6,7},{7,4},{8,9},{9,10},{10,1... | collective-permute-start | bytes 1572872 | tf_op jit(solution)/shard_map/ppermute | solution.py:592
  95.2 113.5 %collective-permute-start.1 = (bf16[128,2048]{1,0:T(8,128)(2,1)}, bf16[128,2048]{1,0:T(8,128)(2,1)}, u32[]{:S(2)}, u32[]{:S(2)}) collective-permute-start(bf16[128,2048]{1,0:T(8,128)(2,1)} %get-tuple-element.39), channel_id=1, source_target_pairs={{0,2},{1,3},{2,0},{3,1},{4,6},{5,7},{6,4},{7,5},{8,10},{9,11},{10,... | collective-permute-start | bytes 1572872 | tf_op jit(solution)/shard_map/ppermute | solution.py:592
  97.6 111.1 %collective-permute-start.2 = (bf16[128,2048]{1,0:T(8,128)(2,1)}, bf16[128,2048]{1,0:T(8,128)(2,1)}, u32[]{:S(2)}, u32[]{:S(2)}) collective-permute-start(bf16[128,2048]{1,0:T(8,128)(2,1)} %get-tuple-element.40), channel_id=1, source_target_pairs={{0,3},{1,0},{2,1},{3,2},{4,7},{5,4},{6,5},{7,6},{8,11},{9,8},{10,9... | collective-permute-start | bytes 1572872 | tf_op jit(solution)/shard_map/ppermute | solution.py:592
  100.3 3.4 %copy-start = (bf16[4,2048,512]{2,1,0:T(8,128)(2,1)S(1)}, bf16[4,2048,512]{2,1,0:T(8,128)(2,1)}, u32[]{:S(2)}) copy-start(bf16[4,2048,512]{2,1,0:T(8,128)(2,1)} %get-tuple-element.26) | copy-start | bytes 25165828
  107.5 0.6 copy-start.9
  108.1 0.7 copy-start.11
  123.0 1.2 copy-start.6
  124.2 1.2 copy-start.12
  146.5 1.3 copy-start.5
  173.7 1.6 copy-start.3
  175.2 21.5 %copy-start.10 = (f32[128,128]{1,0:T(8,128)S(1)}, f32[128,128]{1,0:T(8,128)}, u32[]{:S(2)}) copy-start(f32[128,128]{1,0:T(8,128)} %copy-done.9) | copy-start | bytes 196612
  176.4 0.7 copy-start.7
  196.8 3.4 %copy-start.1 = (bf16[4,2048,512]{2,1,0:T(8,128)(2,1)S(1)}, bf16[4,2048,512]{2,1,0:T(8,128)(2,1)}, u32[]{:S(2)}) copy-start(bf16[4,2048,512]{2,1,0:T(8,128)(2,1)} %get-tuple-element.26) | copy-start | bytes 25165828
  200.2 0.9 copy-start.8
  201.1 7.6 %copy-start.4 = (bf16[2048,512]{1,0:T(8,128)(2,1)S(1)}, bf16[2048,512]{1,0:T(8,128)(2,1)}, u32[]{:S(2)}) copy-start(bf16[2048,512]{1,0:T(8,128)(2,1)} %w_ref.1) | copy-start | bytes 6291460
  201.1 7.7 %copy-start.13 = (bf16[4,128,512]{2,1,0:T(8,128)(2,1)S(1)}, bf16[4,128,512]{2,1,0:T(8,128)(2,1)}, u32[]{:S(2)}) copy-start(bf16[4,128,512]{2,1,0:T(8,128)(2,1)} %get-tuple-element.35.raw_ref) | copy-start | bytes 1572868
  201.1 7.7 %copy-start.14 = (f32[4,128,128]{2,1,0:T(8,128)S(1)}, f32[4,128,128]{2,1,0:T(8,128)}, u32[]{:S(2)}) copy-start(f32[4,128,128]{2,1,0:T(8,128)} %get-tuple-element.36.inv_ref) | copy-start | bytes 786436

commit v3 on v2

--- a/solution.py
+++ b/solution.py
@@ -488,16 +488,21 @@
     )(raw, weight, x, inv, gain)
 
 
-def own_kernel(n, z_ref, raw_ref, inv_ref, w_ref, gain_ref, *refs):
-    pieces, (wg_ref, gg_ref) = refs[:n], refs[n:]
-    z = z_ref[0]
+def to_all_shards(array):
+    n = lax.axis_size("shard")
+    return [array] + [
+        lax.ppermute(array, "shard", [(i, (i + k) % n) for i in range(n)]) for k in range(1, n)
+    ]
+
+
+def own_kernel(n, z_ref, w_ref, gain_ref, *refs):
+    raws, invs, pieces, (wg_ref, gg_ref) = refs[:n], refs[n : 2 * n], refs[2 * n : 3 * n], refs[3 * n :]
     gain = gain_ref[...].astype(F32)
     weight = w_ref[...]
     weight_sum = None
     for k in range(n):
-        source = lax.rem(z + n - k, n)
-        raw = raw_ref[source]
-        inv = inv_ref[source][:, :1]
+        raw = raws[k][...]
+        inv = invs[k][:, :1]
         normed = pieces[k][...].astype(F32) * inv
         term = dot_tn((normed * gain).astype(BF16), raw).astype(BF16).astype(F32)
         grad = dot_nt(raw, weight).astype(BF16).astype(F32)
@@ -509,11 +514,12 @@
 
 
 def own_weight(z, raw_all, inv_all, weight, gain, pieces):
-    n, rows, kw = raw_all.shape
+    n = len(raw_all)
+    rows, kw = raw_all[0].shape
     slice_w = weight.shape[0]
     chunk = min(256, slice_w)
     steps = slice_w // chunk
-    whole = lambda c, zr: (0, 0, 0)
+    whole = lambda c, zr: (0, 0)
     return pl.pallas_call(
         functools.partial(own_kernel, n),
         out_shape=[
@@ -524,11 +530,11 @@
             num_scalar_prefetch=1,
             grid=(steps,),
             in_specs=[
-                pl.BlockSpec(raw_all.shape, whole),
-                pl.BlockSpec(inv_all.shape, whole),
                 pl.BlockSpec((chunk, kw), lambda c, zr: (c, 0)),
                 pl.BlockSpec((1, chunk), lambda c, zr: (0, zr[0] * steps + c)),
             ]
+            + [pl.BlockSpec((rows, kw), whole)] * n
+            + [pl.BlockSpec(inv_all[0].shape, whole)] * n
             + [pl.BlockSpec((rows, chunk), lambda c, zr: (0, c))] * n,
             out_specs=[
                 pl.BlockSpec((chunk, kw), lambda c, zr: (c, 0)),
@@ -539,7 +545,7 @@
         cost_estimate=pl.CostEstimate(
             flops=4 * n * rows * slice_w * kw, bytes_accessed=12 * slice_w * kw, transcendentals=0
         ),
-    )(z.reshape(1), raw_all, inv_all, weight, gain, *pieces)
+    )(z.reshape(1), weight, gain, *raw_all, *inv_all, *pieces)
 
 
 def local(
@@ -578,8 +584,9 @@
         pick, queries[0], logp_grad[0], weight_tok[:, None], block_rows, dp_size
     )
     slot_tile = jnp.broadcast_to(slot_list[:, None], (blocks_dev, 128))
-    incoming, table, all_values, full_weight = exchange(
-        "dp", [outgoing, slot_tile, values[0]], ["a2a", "ag", "ag"], 1, weight=key_weight
+    incoming = lax.all_to_all(outgoing, "dp", split_axis=0, concat_axis=0, tiled=True)
+    table, all_values, full_weight = exchange(
+        "dp", [slot_tile, values[0]], ["ag", "ag"], 1, weight=key_weight
     )
     full_weight = full_weight.reshape(width, key_width)
 
@@ -596,6 +603,7 @@
     gain_row = norm_gain[None, :]
     cos, sin = (t[:, 0, :] for t in rope_tables(position, HD))
     key_rows, inv_tile = make_keys(hidden_in[0], full_weight, gain_row, cos, sin)
+    inv_all = to_all_shards(inv_tile)
     (all_keys,) = exchange("dp", [key_rows], ["ag"], 2)
 
     slot_table = table[:, :, 0].reshape(-1)
@@ -617,7 +625,7 @@
     )
     (parts,) = exchange("dp", [kv_part.reshape(dp_size, row_count, 2 * key_width)], ["a2a"], 3)
     raw_grad, value_grad = make_raw(parts, cos, sin)
-    raw_all, inv_all = exchange("shard", [raw_grad, inv_tile], ["ag", "ag"], 4)
+    raw_all = to_all_shards(raw_grad)
     input_grad = own_rows(raw_grad, full_weight, hidden_in[0], inv_tile, gain_row)
     weight_grad, gain_grad = own_weight(z, raw_all, inv_all, key_weight, gain_row, pieces)
     return (

time: 220 us -> 203 us (0.923)
  Pallas kernels: 192 us -> 165 us
  starting transfers between devices: 4.36 us -> 18 us
    pallas_call x4 -> x3, Pallas kernels: 142 us -> 116 us  [exchange(): pl.pallas_call(functools.partial(exchange_kernel, axis, n, tuple(modes),...]
    ppermute x0 -> x6, starting transfers between devices: none -> 8.56 us  [to_all_shards(): lax.ppermute(array, 'shard', [(i, (i + k) % n) for i in range(n)])]
    all_to_all x0 -> x1, starting transfers between devices: none -> 5.3 us  [local(): lax.all_to_all(outgoing, 'dp', split_axis=0, concat_axis=0, tiled=True)]
    unnamed x38 -> x26, local copies, waits for them, and re-layouts: 15 us -> 12.8 us
  transfers between devices with their start and end apart: 3 -> 10, of which waited for: 0 -> 0; matrix products, arithmetic and copies ran while one was open for 1% -> 2% of each run, Pallas kernels for 43% -> 74%
where the time goes in v3:
time: 203 us; the launch traced here: 202 us
  Pallas kernels  165 us (81%)
  starting transfers between devices  18 us (9%)
  local copies, waits for them, and re-layouts  15.7 us (8%)
  other arithmetic  2.96 us (1%)
    pallas_call x3, Pallas kernels, exchange(): pl.pallas_call(functools.partial(exchange_kernel, axis, n, tuple(modes),...  116 us
    pallas_call x1, Pallas kernels, attend(): pl.pallas_call(functools.partial(attend_kernel, windows), out_shape=[jax....  20.3 us
    unnamed x26, local copies, waits for them, and re-layouts  12.8 us
    pallas_call x1, Pallas kernels, own_weight(): pl.pallas_call(functools.partial(own_kernel, n), out_shape=[jax.ShapeDtyp...  9.15 us
    ppermute x6, starting transfers between devices, to_all_shards(): lax.ppermute(array, 'shard', [(i, (i + k) % n) for i in range(n)])  8.56 us
    pallas_call x1, Pallas kernels, own_rows(): pl.pallas_call(rows_kernel, out_shape=jax.ShapeDtypeStruct((rows, width),...  7.63 us
    pallas_call x1, Pallas kernels, pack_rows(): pl.pallas_call(pack_kernel, out_shape=jax.ShapeDtypeStruct((dp_size, bloc...  6.71 us
    all_to_all x1, starting transfers between devices, local(): lax.all_to_all(outgoing, 'dp', split_axis=0, concat_axis=0, tiled=True)  5.3 us
  transfers between devices with their start and end apart: 10, of which 0 were waited for; matrix products, arithmetic and copies ran while one was open for 2% of the time, Pallas kernels for 74%

profile of v3, /device:TPU:0, one launch (start us, length us, event | category | flops | bytes accessed | tf_op | source)
XLA Modules:
  0.0 202.1 jit_solution(11311534159453481841)
XLA Ops:
  1.3 0.7 copy.17.w_ref
  3.3 6.7 %shard_map.138 = bf16[8,16,8192]{2,1,0:T(8,128)(2,1)} custom-call(s32[8]{0:T(128)} %select_reduce_fusion.1.pick_ref, bf16[128,4096]{1,0:T(8,128)(2,1)} %bitcast.45, bf16[128,4096]{1,0:T(8,128)(2,1)} %bitcast.46, f32[128,1]{1,0:T(8,128)} %copy.17.w_ref), custom_call_target="tpu_custom_call" | custom-call | bytes 4194304 | tf_op jit(solution)/shard_map/pallas_call | solution.py:219
  10.1 5.3 %all-to-all-start = ((bf16[8,16,8192]{2,1,0:T(8,128)(2,1)}), bf16[8,16,8192]{2,1,0:T(8,128)(2,1)}, u32[]{:S(2)}, u32[]{:S(2)}) async-start(bf16[8,16,8192]{2,1,0:T(8,128)(2,1)} %shard_map.138), calls=%async_computation | async-start | bytes 4194304 | tf_op jit(solution)/shard_map/all_to_all | solution.py:587
  15.4 1.2 dynamic-slice_bitcast_fusion
  17.3 73.8 %shard_map.137 = (s32[8,8,128]{2,1,0:T(8,128)}, bf16[8,128,512]{2,1,0:T(8,128)(2,1)}, bf16[4,2048,512]{2,1,0:T(8,128)(2,1)}) custom-call(s32[8,128]{1,0:T(8,128)} %broadcast_in_dim.81.refs_0_, bf16[128,512]{1,0:T(8,128)(2,1)} %bitcast.47, bf16[2048,512]{1,0:T(8,128)(2,1)} %w_ref.1), custom_call_target="tpu_custom_call" | custom-call | bytes 189399040 | tf_op jit(solution)/shard_map/pallas_call | solution.py:198
  91.8 3.4 %copy-done = bf16[4,2048,512]{2,1,0:T(8,128)(2,1)S(1)} copy-done((bf16[4,2048,512]{2,1,0:T(8,128)(2,1)S(1)}, bf16[4,2048,512]{2,1,0:T(8,128)(2,1)}, u32[]{:S(2)}) %copy-start) | copy-done | bytes 8388632
  95.2 3.8 %shard_map.139 = (bf16[128,512]{1,0:T(8,128)(2,1)S(1)}, f32[128,128]{1,0:T(8,128)S(1)}) custom-call(bf16[128,8192]{1,0:T(8,128)(2,1)S(1)} %bitcast.39, bf16[8192,512]{1,0:T(8,128)(2,1)S(1)} %bitcast.37, bf16[1,8192]{1,0:T(2,128)(2,1)S(1)} %broadcast_in_dim.86.gain_ref, f32[128,64]{1,0:T(8,128)S(1)} %get-tuple-element.42.cos_ref, ...), custom_call_target="tpu_custom_call" | custom-call | flops 1073741824 | bytes 16777216 | tf_op jit(solution)/shard_map/pallas_call | solution.py:390
  99.6 0.7 collective-permute-start.3
  100.4 2.6 %collective-permute-start.4 = (f32[128,128]{1,0:T(8,128)S(1)}, f32[128,128]{1,0:T(8,128)S(1)}, u32[]{:S(2)}, u32[]{:S(2)}) collective-permute-start(f32[128,128]{1,0:T(8,128)S(1)} %get-tuple-element.28.inv_ref.refs_4_), channel_id=1, source_target_pairs={{0,2},{1,3},{2,0},{3,1},{4,6},{5,7},{6,4},{7,5},{8,10},{9,11},{10,... | collective-permute-start | bytes 196616 | tf_op jit(solution)/shard_map/ppermute | solution.py:494
  103.0 1.3 collective-permute-start.5
  105.5 15.0 %shard_map.140 = bf16[8,128,512]{2,1,0:T(8,128)(2,1)} custom-call(bf16[128,512]{1,0:T(8,128)(2,1)} %copy-done.7), custom_call_target="tpu_custom_call" | custom-call | bytes 20971520 | tf_op jit(solution)/shard_map/pallas_call | solution.py:198
  121.2 3.0 %collective-permute-start.8 = (bf16[128,2048]{1,0:T(8,128)(2,1)}, bf16[128,2048]{1,0:T(8,128)(2,1)}, u32[]{:S(2)}, u32[]{:S(2)}) collective-permute-start(bf16[128,2048]{1,0:T(8,128)(2,1)} %get-tuple-element.34), channel_id=1, source_target_pairs={{0,3},{1,0},{2,1},{3,2},{4,7},{5,4},{6,5},{7,6},{8,11},{9,8},{10,9... | collective-permute-start | bytes 1572872 | tf_op jit(solution)/shard_map/ppermute | solution.py:599
  124.2 1.2 copy-done.6
  125.4 1.2 copy-done.8
  126.6 20.3 %shard_map.141 = (bf16[128,4096]{1,0:T(8,128)(2,1)}, bf16[1024,1024]{1,0:T(8,128)(2,1)S(1)}) custom-call(s32[8]{0:T(128)S(1)} %get-tuple-element.44.src_ref, s32[8]{0:T(128)S(1)} %get-tuple-element.43.row_ref, s32[8]{0:T(128)S(1)} %select_reduce_fusion.2.low_ref, s32[8]{0:T(128)S(1)} %get-tuple-element.45.starts_ref, ...), custom_call_target="tpu_custom_call" | custom-call | flops 20000000000 | bytes 60000000 | tf_op jit(solution)/shard_map/pallas_call | solution.py:326
  146.9 1.3 copy-done.5
  148.2 27.1 %shard_map.142.parts_ref = bf16[8,128,1024]{2,1,0:T(8,128)(2,1)} custom-call(bf16[8,128,1024]{2,1,0:T(8,128)(2,1)} %bitcast.41), custom_call_target="tpu_custom_call" | custom-call | bytes 41943040 | tf_op jit(solution)/shard_map/pallas_call | solution.py:198
  175.3 1.6 copy-done.3
  176.9 1.1 shard_map.143
  178.1 0.7 collective-permute-start.1
  178.8 3.1 %collective-permute-start.2 = (bf16[128,512]{1,0:T(8,128)(2,1)S(1)}, bf16[128,512]{1,0:T(8,128)(2,1)S(1)}, u32[]{:S(2)}, u32[]{:S(2)}) collective-permute-start(bf16[128,512]{1,0:T(8,128)(2,1)S(1)} %get-tuple-element.27.raw_ref.refs_0_), channel_id=1, source_target_pairs={{0,3},{1,0},{2,1},{3,2},{4,7},{5,4},{6,5},{7,6},{8,11},{9,8},{10,9... | collective-permute-start | bytes 393224 | tf_op jit(solution)/shard_map/ppermute | solution.py:494
  181.9 3.4 %copy-done.1 = bf16[4,2048,512]{2,1,0:T(8,128)(2,1)S(1)} copy-done((bf16[4,2048,512]{2,1,0:T(8,128)(2,1)S(1)}, bf16[4,2048,512]{2,1,0:T(8,128)(2,1)}, u32[]{:S(2)}) %copy-start.1) | copy-done | bytes 8388632
  185.3 7.6 %shard_map.144 = bf16[128,8192]{1,0:T(8,128)(2,1)} custom-call(bf16[128,512]{1,0:T(8,128)(2,1)S(1)} %get-tuple-element.27.raw_ref.refs_0_, bf16[8192,512]{1,0:T(8,128)(2,1)S(1)} %bitcast.38, bf16[128,8192]{1,0:T(8,128)(2,1)S(1)} %bitcast.40, f32[128,128]{1,0:T(8,128)S(1)} %get-tuple-element.28.inv_ref.refs_4_, bf16[1,8192]{1,0:T(2,128)(2,1)S(1)} %broadcast_in_dim.86.gain_ref), custom_call_target="tpu_custom_call" | custom-call | flops 1073741824 | bytes 16777216 | tf_op jit(solution)/shard_map/pallas_call | solution.py:471
  193.0 9.2 %shard_map.145 = (f32[2048,512]{1,0:T(8,128)}, f32[1,2048]{1,0:T(1,128)}) custom-call(s32[1]{0:T(128)} %bitcast.23.z_ref, bf16[2048,512]{1,0:T(8,128)(2,1)S(1)} %copy-done.4, bf16[1,8192]{1,0:T(2,128)(2,1)S(1)} %broadcast_in_dim.86.gain_ref, bf16[128,512]{1,0:T(8,128)(2,1)S(1)} %get-tuple-element.27.raw_ref.refs_0_, ...), custom_call_target="tpu_custom_call" | custom-call | flops 2147483648 | bytes 12582912 | tf_op jit(solution)/shard_map/pallas_call | solution.py:523
  (51 shorter events, 5.8 us)
Async XLA Ops:
  10.1 5.3 %copy-start.2 = (bf16[1,128,8192]{2,1,0:T(8,128)(2,1)S(1)}, bf16[1,128,8192]{2,1,0:T(8,128)(2,1)}, u32[]{:S(2)}) copy-start(bf16[1,128,8192]{2,1,0:T(8,128)(2,1)} %param.10) | copy-start | bytes 6291460
  10.1 114.1 %all-to-all-start = ((bf16[8,16,8192]{2,1,0:T(8,128)(2,1)}), bf16[8,16,8192]{2,1,0:T(8,128)(2,1)}, u32[]{:S(2)}, u32[]{:S(2)}) async-start(bf16[8,16,8192]{2,1,0:T(8,128)(2,1)} %shard_map.138), calls=%async_computation | async-start | bytes 4194304 | tf_op jit(solution)/shard_map/all_to_all | solution.py:587
  15.4 1.2 copy-start.11
  16.6 74.5 %copy-start.12 = (s32[1,8]{1,0:T(1,128)S(1)}, s32[1,8]{1,0:T(1,128)}, u32[]{:S(2)}) copy-start(s32[1,8]{1,0:T(1,128)} %param.18) | copy-start | bytes 100
  16.6 74.7 %copy-start.10 = (bf16[8192]{0:T(1024)(128)(2,1)S(1)}, bf16[8192]{0:T(1024)(128)(2,1)}, u32[]{:S(2)}) copy-start(bf16[8192]{0:T(1024)(128)(2,1)} %param.11) | copy-start | bytes 49156
  91.8 3.4 %copy-start = (bf16[4,2048,512]{2,1,0:T(8,128)(2,1)S(1)}, bf16[4,2048,512]{2,1,0:T(8,128)(2,1)}, u32[]{:S(2)}) copy-start(bf16[4,2048,512]{2,1,0:T(8,128)(2,1)} %get-tuple-element.22) | copy-start | bytes 25165828
  95.2 25.3 %copy-start.9 = (s32[8,8,128]{2,1,0:T(8,128)S(1)}, s32[8,8,128]{2,1,0:T(8,128)}, u32[]{:S(2)}) copy-start(s32[8,8,128]{2,1,0:T(8,128)} %get-tuple-element.21) | copy-start | bytes 98308
  99.0 0.7 copy-start.7
  99.6 21.6 %collective-permute-start.3 = (f32[128,128]{1,0:T(8,128)S(1)}, f32[128,128]{1,0:T(8,128)S(1)}, u32[]{:S(2)}, u32[]{:S(2)}) collective-permute-start(f32[128,128]{1,0:T(8,128)S(1)} %get-tuple-element.28.inv_ref.refs_4_), channel_id=1, source_target_pairs={{0,1},{1,2},{2,3},{3,0},{4,5},{5,6},{6,7},{7,4},{8,9},{9,10},{10,1... | collective-permute-start | bytes 196616 | tf_op jit(solution)/shard_map/ppermute | solution.py:494
  100.4 77.7 %collective-permute-start.4 = (f32[128,128]{1,0:T(8,128)S(1)}, f32[128,128]{1,0:T(8,128)S(1)}, u32[]{:S(2)}, u32[]{:S(2)}) collective-permute-start(f32[128,128]{1,0:T(8,128)S(1)} %get-tuple-element.28.inv_ref.refs_4_), channel_id=1, source_target_pairs={{0,2},{1,3},{2,0},{3,1},{4,6},{5,7},{6,4},{7,5},{8,10},{9,11},{10,... | collective-permute-start | bytes 196616 | tf_op jit(solution)/shard_map/ppermute | solution.py:494
  103.0 75.1 %collective-permute-start.5 = (f32[128,128]{1,0:T(8,128)S(1)}, f32[128,128]{1,0:T(8,128)}, u32[]{:S(2)}, u32[]{:S(2)}) collective-permute-start(f32[128,128]{1,0:T(8,128)S(1)} %get-tuple-element.28.inv_ref.refs_4_), channel_id=1, source_target_pairs={{0,3},{1,0},{2,1},{3,2},{4,7},{5,4},{6,5},{7,6},{8,11},{9,8},{10,9... | collective-permute-start | bytes 196616 | tf_op jit(solution)/shard_map/ppermute | solution.py:494
  104.3 74.5 %collective-permute-start.6 = (bf16[128,2048]{1,0:T(8,128)(2,1)}, bf16[128,2048]{1,0:T(8,128)(2,1)S(1)}, u32[]{:S(2)}, u32[]{:S(2)}) collective-permute-start(bf16[128,2048]{1,0:T(8,128)(2,1)} %get-tuple-element.32), channel_id=1, source_target_pairs={{0,1},{1,2},{2,3},{3,0},{4,5},{5,6},{6,7},{7,4},{8,9},{9,10},{10,1... | collective-permute-start | bytes 1572872 | tf_op jit(solution)/shard_map/ppermute | solution.py:599
  105.0 88.0 %collective-permute-start.7 = (bf16[128,2048]{1,0:T(8,128)(2,1)}, bf16[128,2048]{1,0:T(8,128)(2,1)}, u32[]{:S(2)}, u32[]{:S(2)}) collective-permute-start(bf16[128,2048]{1,0:T(8,128)(2,1)} %get-tuple-element.33), channel_id=1, source_target_pairs={{0,2},{1,3},{2,0},{3,1},{4,6},{5,7},{6,4},{7,5},{8,10},{9,11},{10,... | collective-permute-start | bytes 1572872 | tf_op jit(solution)/shard_map/ppermute | solution.py:599
  121.2 71.8 %collective-permute-start.8 = (bf16[128,2048]{1,0:T(8,128)(2,1)}, bf16[128,2048]{1,0:T(8,128)(2,1)}, u32[]{:S(2)}, u32[]{:S(2)}) collective-permute-start(bf16[128,2048]{1,0:T(8,128)(2,1)} %get-tuple-element.34), channel_id=1, source_target_pairs={{0,3},{1,0},{2,1},{3,2},{4,7},{5,4},{6,5},{7,6},{8,11},{9,8},{10,9... | collective-permute-start | bytes 1572872 | tf_op jit(solution)/shard_map/ppermute | solution.py:599
  124.2 1.2 copy-start.6
  125.4 1.2 copy-start.8
  146.9 1.3 copy-start.5
  175.3 1.6 copy-start.3
  176.9 16.1 %copy-start.4 = (bf16[2048,512]{1,0:T(8,128)(2,1)S(1)}, bf16[2048,512]{1,0:T(8,128)(2,1)}, u32[]{:S(2)}) copy-start(bf16[2048,512]{1,0:T(8,128)(2,1)} %w_ref.1) | copy-start | bytes 6291460
  178.0 14.9 %collective-permute-start = (bf16[128,512]{1,0:T(8,128)(2,1)S(1)}, bf16[128,512]{1,0:T(8,128)(2,1)S(1)}, u32[]{:S(2)}, u32[]{:S(2)}) collective-permute-start(bf16[128,512]{1,0:T(8,128)(2,1)S(1)} %get-tuple-element.27.raw_ref.refs_0_), channel_id=1, source_target_pairs={{0,1},{1,2},{2,3},{3,0},{4,5},{5,6},{6,7},{7,4},{8,9},{9,10},{10,1... | collective-permute-start | bytes 393224 | tf_op jit(solution)/shard_map/ppermute | solution.py:494
  178.1 14.9 %collective-permute-start.1 = (bf16[128,512]{1,0:T(8,128)(2,1)S(1)}, bf16[128,512]{1,0:T(8,128)(2,1)S(1)}, u32[]{:S(2)}, u32[]{:S(2)}) collective-permute-start(bf16[128,512]{1,0:T(8,128)(2,1)S(1)} %get-tuple-element.27.raw_ref.refs_0_), channel_id=1, source_target_pairs={{0,2},{1,3},{2,0},{3,1},{4,6},{5,7},{6,4},{7,5},{8,10},{9,11},{10,... | collective-permute-start | bytes 393224 | tf_op jit(solution)/shard_map/ppermute | solution.py:494
  178.8 14.2 %collective-permute-start.2 = (bf16[128,512]{1,0:T(8,128)(2,1)S(1)}, bf16[128,512]{1,0:T(8,128)(2,1)S(1)}, u32[]{:S(2)}, u32[]{:S(2)}) collective-permute-start(bf16[128,512]{1,0:T(8,128)(2,1)S(1)} %get-tuple-element.27.raw_ref.refs_0_), channel_id=1, source_target_pairs={{0,3},{1,0},{2,1},{3,2},{4,7},{5,4},{6,5},{7,6},{8,11},{9,8},{10,9... | collective-permute-start | bytes 393224 | tf_op jit(solution)/shard_map/ppermute | solution.py:494
  181.9 3.4 %copy-start.1 = (bf16[4,2048,512]{2,1,0:T(8,128)(2,1)S(1)}, bf16[4,2048,512]{2,1,0:T(8,128)(2,1)}, u32[]{:S(2)}) copy-start(bf16[4,2048,512]{2,1,0:T(8,128)(2,1)} %get-tuple-element.22) | copy-start | bytes 25165828
